TPU v7x, 32 devices: a whole 2x2x4 slice. The times are simulated.
32 devices in a mesh: outer: 4 (over y, core), inner: 8 (over z, x).
Axes of the slice: x: 2, y: 2, z: 4, core: 2. Of those that a mesh axis runs over, the one named last changes fastest.
Arguments:
- layer_input: bfloat16 [1024, 256, 192], P(('outer', 'inner')), may hold values from -6 to 6
- out_grad: bfloat16 [1024, 256, 192], P(('outer', 'inner')), may hold values from -6 to 6
- mix_weight: bfloat16 [256, 128], replicated, may hold values from -0.375 to 0.375
- lift_weight: bfloat16 [128, 192], replicated, may hold values from -0.5 to 0.5
- linear_weight: bfloat16 [256, 256], replicated, may hold values from -0.375 to 0.375
- row_ids: int32 [1024, 256], P(('outer', 'inner')), may hold values from 0 to 16383, as said below
- row_home: int32 [16384], replicated, may hold values from 0 to 16383, as said below
- table: float32 [16384, 192], P('inner'), may hold values from -0.6 to 0.6
- row_accum: float32 [16384], P('inner'), may hold values from 1 to 100
Outputs:
- new_table: float32 [16384, 192], P('inner')
- new_accum: float32 [16384], P('inner')
- mix_grad: float32 [256, 128], replicated
- lift_grad: float32 [128, 192], replicated
- linear_grad: float32 [256, 256], replicated
Inputs may be any that keep to these rules, and one draw needn't show every extreme that they name: row_home is a permutation: hashed row i is stored at position row_home[i], held by inner index row_home[i] // 2048. In each aligned block of 16 samples (all their features together), every inner index is the owner, row_home[row_ids] // 2048, of exactly 512 lookups. The same row may be named many times.
All inputs are finite; a program needn't handle non-finite values.
Results may differ from a plain program's by a relative error of at most 0.0041.
Values may be sent and summed in bfloat16 or wider, within the bound.
No kernel may reach another device: no remote copies, remote signals or barrier semaphores. Data moves between devices by JAX's collectives and lax.ppermute only.
A program may use at most 64 MiB of HBM per device.

v0:
```python
import functools
import math

import jax
import jax.numpy as jnp
from jax import lax
from jax.experimental import pallas as pl
from jax.experimental.pallas import tpu as pltpu
from jax.sharding import PartitionSpec as P

LEARN_RATE = 0.5


def interaction_grads(inputs, cotangent, mix_weight, lift_weight, linear_weight, scaling):
    compressed = jnp.einsum(
        "bfd,fk->bdk", inputs, mix_weight, preferred_element_type=jnp.float32
    ).astype(jnp.bfloat16)
    products = (
        jnp.einsum("bfd,bdk->bfk", inputs, compressed, preferred_element_type=jnp.float32) * scaling
    ).astype(jnp.bfloat16)
    d_products = jnp.einsum(
        "bfd,kd->bfk", cotangent, lift_weight, preferred_element_type=jnp.float32
    ).astype(jnp.bfloat16)
    d_compressed = (
        jnp.einsum("bfd,bfk->bdk", inputs, d_products, preferred_element_type=jnp.float32) * scaling
    ).astype(jnp.bfloat16)
    d_inputs = cotangent.astype(jnp.float32)
    d_inputs = d_inputs + jnp.einsum(
        "fg,bfd->bgd", linear_weight, cotangent, preferred_element_type=jnp.float32
    )
    d_inputs = d_inputs + scaling * jnp.einsum(
        "bfk,bdk->bfd", d_products, compressed, preferred_element_type=jnp.float32
    )
    d_inputs = d_inputs + jnp.einsum(
        "fk,bdk->bfd", mix_weight, d_compressed, preferred_element_type=jnp.float32
    )
    g_mix = jnp.einsum("bfd,bdk->fk", inputs, d_compressed, preferred_element_type=jnp.float32)
    g_lift = jnp.einsum("bfk,bfd->kd", products, cotangent, preferred_element_type=jnp.float32)
    g_linear = jnp.einsum("bfd,bgd->fg", cotangent, inputs, preferred_element_type=jnp.float32)
    rows_out = d_inputs.astype(jnp.bfloat16).reshape(-1, d_inputs.shape[2])
    return (rows_out, (g_mix, g_lift, g_linear))


def adagrad(weights, history, gradient):
    updated = history + jnp.mean(gradient * gradient, axis=1)
    return (weights - LEARN_RATE * gradient / jnp.sqrt(updated)[:, None], updated)


def owner_ranks(owner_of, owners):
    lookups = owner_of.shape[0]
    width = math.gcd(lookups, 128)
    groups = lookups // width
    hot = (owner_of[:, None] == jnp.arange(owners, dtype=jnp.int32)[None, :]).astype(jnp.bfloat16)
    hot = hot.reshape(groups, width, owners)
    lower = (jnp.arange(width)[:, None] > jnp.arange(width)[None, :]).astype(jnp.bfloat16)
    within = jnp.einsum("ij,gjo->gio", lower, hot, preferred_element_type=jnp.float32)
    totals = jnp.sum(hot.astype(jnp.float32), axis=1)
    before = jnp.cumsum(totals, axis=0) - totals
    counted = jnp.sum(hot.astype(jnp.float32) * (within + before[:, None, :]), axis=2)
    return counted.reshape(-1).astype(jnp.int32)


def add_rows(collected, slots, values):
    count = values.shape[0]
    table_rows = collected.shape[0]
    width = math.gcd(count, 2048)
    columns = jnp.arange(table_rows, dtype=jnp.int32)
    for block_index in range(count // width):
        start = block_index * width
        hot = (slots[start : start + width, None] == columns[None, :]).astype(jnp.bfloat16)
        collected = collected + jnp.einsum(
            "lr,ld->rd", hot, values[start : start + width], preferred_element_type=jnp.float32
        )
    return collected


def routed_rows(
    layer_input,
    out_grad,
    mix_weight,
    lift_weight,
    linear_weight,
    row_ids,
    row_home,
    table,
    row_accum,
):
    owners = lax.axis_size("inner")
    sample_count, feature_count, embed_width = layer_input.shape
    table_rows = table.shape[0]
    half_samples = sample_count // 2
    lookups = sample_count * feature_count
    per_owner = lookups // (2 * owners)
    scaling = 1.0 / math.sqrt(embed_width)
    placed = jnp.take(row_home, row_ids.reshape(-1), axis=0)
    owner_of = placed // table_rows
    target = owner_of * (2 * per_owner) + owner_ranks(owner_of, owners)
    ordering = jnp.zeros((lookups,), jnp.int32).at[target].set(jnp.arange(lookups, dtype=jnp.int32))
    ordering = ordering.reshape(owners, 2, per_owner)
    local_rows = (
        jnp.zeros((lookups,), jnp.int32)
        .at[target]
        .set(placed % table_rows)
        .reshape(owners, 2 * per_owner)
    )
    arrived_rows = lax.all_to_all(
        local_rows, "inner", split_axis=0, concat_axis=0, tiled=True
    ).reshape(owners, 2, per_owner)
    collected = jnp.zeros((table_rows, embed_width), jnp.float32)
    totals = None
    for half_index in range(2):
        first_sample = half_index * half_samples
        rows_out, partial_value = interaction_grads(
            layer_input[first_sample : first_sample + half_samples],
            out_grad[first_sample : first_sample + half_samples],
            mix_weight,
            lift_weight,
            linear_weight,
            scaling,
        )
        picked = ordering[:, half_index, :] - half_index * half_samples * feature_count
        outgoing = jnp.take(rows_out, picked.reshape(-1), axis=0).reshape(
            owners, per_owner, embed_width
        )
        incoming = lax.all_to_all(outgoing, "inner", split_axis=0, concat_axis=0, tiled=True)
        collected = add_rows(
            collected, arrived_rows[:, half_index, :].reshape(-1), incoming.reshape(-1, embed_width)
        )
        if totals is None:
            totals = partial_value
        else:
            totals = tuple((earlier + later for earlier, later in zip(totals, partial_value)))
    batch_total = sample_count * lax.axis_size("outer") * owners
    summed = lax.psum((totals[0], totals[1], totals[2]), ("outer", "inner"))
    mix_grad = summed[0] / batch_total
    lift_grad = summed[1] / batch_total
    linear_grad = summed[2] / batch_total
    complete = lax.psum(collected, "outer")
    new_table, new_accum = adagrad(table, row_accum, complete)
    return (new_table, new_accum, mix_grad, lift_grad, linear_grad)


def matmul(left, right):
    return jnp.dot(left, right, preferred_element_type=jnp.float32)


def matmul_nt(left, right):
    return lax.dot_general(left, right, (((1,), (1,)), ((), ())), preferred_element_type=jnp.float32)


def one_hot(matches):
    return jnp.where(matches, 1.0, 0.0).astype(jnp.bfloat16)


def place_kernel(shift, owners, ids_ref, home_ref, rank_ref, slot_ref, count_ref):
    samples, feats = ids_ref.shape
    high, low = home_ref.shape
    half = low // 2
    home = home_ref[...]
    pieces = []
    for part in (home & 255, home >> 8):
        down = part.astype(jnp.float32).T
        pieces.append(jnp.concatenate([down[:half], down[half:]], axis=1))
    pieces = jnp.concatenate(pieces, axis=0).astype(jnp.bfloat16)
    high_at = lax.broadcasted_iota(jnp.int32, (2 * high, feats), 0)
    low_at = lax.broadcasted_iota(jnp.int32, (half, feats), 0)
    lane = lax.broadcasted_iota(jnp.int32, (1, feats), 1)
    count_lane = lax.broadcasted_iota(jnp.int32, (8, 128), 1)

    @pl.loop(0, samples // 8)
    def _(group):
        first = pl.multiple_of(group * 8, 8)
        ids = ids_ref[pl.ds(first, 8), :]
        every = range(8)
        ones = [ids[row : row + 1] for row in every]
        hots = [one_hot(high_at == ((one >> 6) & 1) * high + (one >> 7)) for one in ones]
        founds = [matmul(pieces, hot) for hot in hots]
        places = []
        for row in every:
            value = founds[row][:half] + 256.0 * founds[row][half:]
            value = jnp.where(low_at == (ones[row] & (half - 1)), value, 0.0)
            places.append(jnp.sum(value, axis=0, keepdims=True))
        place = jnp.concatenate(places, axis=0).astype(jnp.int32)
        owner_all = place >> shift
        slot_ref[pl.ds(first, 8), :] = place & ((1 << shift) - 1)
        keys = (owner_all * feats + lane).astype(jnp.float32)
        downs = [jnp.broadcast_to(keys[row : row + 1], (128, feats)).T for row in every]
        ranks = []
        for row in every:
            parts = []
            for at in range(0, feats, 128):
                less = downs[row] < keys[row : row + 1, at : at + 128]
                parts.append(jnp.sum(jnp.where(less, 1.0, 0.0), axis=0, keepdims=True))
            ranks.append(jnp.concatenate(parts, axis=1))
        rank_ref[pl.ds(first, 8), :] = jnp.concatenate(ranks, axis=0).astype(jnp.int32)
        counts = jnp.zeros((8, 128), jnp.float32)
        for owner_at in range(owners):
            number = jnp.sum(jnp.where(owner_all == owner_at, 1.0, 0.0), axis=1, keepdims=True)
            counts = jnp.where(count_lane == owner_at, number, counts)
        most = jnp.max(counts, axis=1, keepdims=True)
        counts = jnp.where(count_lane == owners, most, counts)
        count_ref[pl.ds(first, 8), :] = counts.astype(jnp.int32)


COPY_ROWS = 56
SCRATCH = 16


def sum_list(values):
    total = values[0]
    for value in values[1:]:
        total = total + value
    return total


def positions():
    return lax.axis_index("outer"), lax.axis_index("inner")


def grads_kernel(
    sizes,
    x_ref,
    g_ref,
    mix_ref,
    lift_ref,
    linear_ref,
    ids_ref,
    home_ref,
    *rest,
):
    group, steps, owners, per_owner, scaling, shift = sizes
    far_count = owners // 4
    keep_refs, send_refs = rest[:far_count], rest[far_count : 2 * far_count]
    rows_ref = rest[2 * far_count]
    dense_refs, scratch = rest[2 * far_count + 1 : -SCRATCH], rest[-SCRATCH:]
    rank_ref, slot_ref, found_ref, count_ref, copied = scratch[:5]
    step = pl.program_id(0)
    outer, inner = positions()

    @pl.when(step == 0)
    def _():
        place_kernel(shift, owners, ids_ref, home_ref, rank_ref, slot_ref, found_ref)
        copy = pltpu.make_async_copy(found_ref, count_ref, copied)
        copy.start()
        copy.wait()

    @pl.when((step > 0) & (step <= steps))
    def _():
        gather_rows(
            step - 1,
            outer,
            sizes,
            count_ref,
            x_ref,
            g_ref,
            mix_ref,
            lift_ref,
            linear_ref,
            rank_ref,
            slot_ref,
            dense_refs,
            *scratch[5:],
        )

    @pl.when(step > steps)
    def _():
        place = owners - 1 - (step - steps - 1)
        row_a, row_b = scratch[-4], scratch[-3]
        near = (step - steps - 1) ^ inner
        rows_ref[0, :, :128] = row_a[near, pl.ds(0, per_owner), :].astype(jnp.bfloat16)
        rows_ref[0, :, 128:] = row_b[near, pl.ds(0, per_owner), :].astype(jnp.bfloat16)
        owner = place ^ inner
        first_rows = row_a[owner, pl.ds(0, per_owner), :]
        second_rows = row_b[owner, pl.ds(0, per_owner), :]
        at = x_ref.shape[1] - 128
        build_rows(at, outer, first_rows, second_rows, place, far_count, keep_refs, send_refs)


def join_rows(count_ref, filled, sorted_a, sorted_b, row_a, row_b, step, group, owners):
    begun = (step >= 0).astype(jnp.int32)
    now = (step + 2) % 2
    first = jnp.maximum(step, 0) * group
    every = range(group)
    numbers = [[count_ref[first + k, owner] * begun for owner in range(owners)] for k in every]
    starts = [filled[owner] for owner in range(owners)]
    ends = list(starts)
    for k in every:
        begin = 0
        for owner in range(owners):
            source, target = pl.ds(begin, COPY_ROWS), pl.ds(ends[owner], COPY_ROWS)
            row_a[owner, target, :] = sorted_a[now, k, source, :]
            row_b[owner, target, :] = sorted_b[now, k, source, :]
            ends[owner] = ends[owner] + numbers[k][owner]
            begin = begin + numbers[k][owner]
    most = count_ref[first, owners] * begun
    for k in range(1, group):
        most = jnp.maximum(most, count_ref[first + k, owners] * begun)

    @pl.when(most > COPY_ROWS)
    def _():
        again = list(starts)
        for k in every:
            begin = 0
            for owner in range(owners):

                def copy(turn, carry, begin=begin, at=again[owner], owner=owner, k=k):
                    off = turn * COPY_ROWS
                    source, target = pl.ds(begin + off, COPY_ROWS), pl.ds(at + off, COPY_ROWS)
                    row_a[owner, target, :] = sorted_a[now, k, source, :]
                    row_b[owner, target, :] = sorted_b[now, k, source, :]
                    return carry

                turns = (numbers[k][owner] + COPY_ROWS - 1) // COPY_ROWS
                lax.fori_loop(0, turns, copy, 0)
                again[owner] = again[owner] + numbers[k][owner]
                begin = begin + numbers[k][owner]

    for owner in range(owners):
        filled[owner] = ends[owner]


def gather_rows(
    step,
    outer,
    sizes,
    count_ref,
    x_ref,
    g_ref,
    mix_ref,
    lift_ref,
    linear_ref,
    rank_ref,
    slot_ref,
    dense_refs,
    mix_down,
    lift_down,
    mix_sum,
    lift_sum,
    linear_sum,
    sorted_a,
    sorted_b,
    row_a,
    row_b,
    dense_ref,
    filled,
):
    group, steps, owners, _, scaling, _ = sizes
    width, feats = x_ref.shape[1:]
    rank = mix_ref.shape[1]

    @pl.when(step == 0)
    def _():
        mix_down[...] = mix_ref[...].astype(jnp.float32).T.astype(jnp.bfloat16)
        lift_down[...] = lift_ref[...].astype(jnp.float32).T.astype(jnp.bfloat16)
        mix_sum[...] = jnp.zeros_like(mix_sum)
        lift_sum[...] = jnp.zeros_like(lift_sum)
        linear_sum[...] = jnp.zeros_like(linear_sum)
        for owner in range(owners):
            filled[owner] = 0

    now = step % 2
    join_rows(count_ref, filled, sorted_a, sorted_b, row_a, row_b, step - 1, group, owners)
    row_at = lax.broadcasted_iota(jnp.int32, (feats, feats), 0)
    extra_at = lax.broadcasted_iota(jnp.int32, (feats - width, feats), 0)
    every = range(group)
    d_prods = [matmul(lift_down[...], g_ref[k]).astype(jnp.bfloat16) for k in every]
    boths = [
        matmul_nt(x_ref[k], jnp.concatenate([mix_down[...], d_prods[k]], axis=0)) for k in every
    ]
    comps = [both[:, :rank].astype(jnp.bfloat16) for both in boths]
    d_comps = [(both[:, rank:] * scaling).astype(jnp.bfloat16) for both in boths]
    x_flat = x_ref[...].reshape(group * width, feats).T
    x_flats = [x_flat[:, k * width : (k + 1) * width] for k in every]
    pairs = [
        matmul(x_flats[k], jnp.concatenate([comps[k], d_comps[k]], axis=1)) for k in every
    ]
    prods = [(pair[:, :rank] * scaling).astype(jnp.bfloat16) for pair in pairs]
    mix_sum[...] += sum_list([pair[:, rank:] for pair in pairs])
    g_all = g_ref[...].reshape(group * width, feats)
    d_all = g_all.astype(jnp.float32) + matmul(g_all, linear_ref[...])
    d_all = d_all + matmul(jnp.concatenate(d_comps, axis=0), mix_down[...])
    d_ins = [
        d_all[k * width : (k + 1) * width] + scaling * matmul(comps[k], d_prods[k]) for k in every
    ]
    moves, rows_downs = [], []
    for k in every:
        slot = slot_ref[pl.ds(step * group + k, 1), :]
        extra = jnp.where(extra_at == 0, slot >> 4, jnp.where(extra_at == 1, slot & 15, 0))
        rows_downs.append(
            jnp.concatenate(
                [d_ins[k].astype(jnp.bfloat16), extra.astype(jnp.float32).astype(jnp.bfloat16)],
                axis=0,
            )
        )
        moves.append(one_hot(row_at == rank_ref[pl.ds(step * group + k, 1), :]))
    for k in every:
        ordered = matmul_nt(moves[k], rows_downs[k])
        sorted_a[now, k, :feats] = ordered[:, :128]
        sorted_b[now, k, :feats] = ordered[:, 128:]
    linear_sum[...] += matmul(x_flat, g_all)
    lift_sum[...] += sum_list([matmul(g_ref[k], prods[k]) for k in every])

    @pl.when(step == steps - 1)
    def _():
        join_rows(count_ref, filled, sorted_a, sorted_b, row_a, row_b, step, group, owners)
        dense_ref[:feats] = mix_sum[...]
        linear = linear_sum[...].T
        for at in range(feats // 128):
            dense_ref[feats * (1 + at) : feats * (2 + at)] = linear[:, 128 * at : 128 * (at + 1)]
        dense_ref[feats * (1 + feats // 128) :] = lift_sum[...]
        piece = dense_refs[0].shape[0]
        for index, ref in enumerate(dense_refs):
            first = pl.multiple_of((index ^ outer) * piece, piece)
            ref[...] = dense_ref[pl.ds(first, piece), :]


def build_rows(at, my_outer, first_rows, second_rows, place, first, keep_refs, send_refs):
    outers, piece = 2 * keep_refs[0].shape[1], keep_refs[0].shape[3]
    per_owner = first_rows.shape[0]
    rows_down = jnp.concatenate([first_rows.T, second_rows.T[:at]], axis=0).astype(jnp.bfloat16)
    slots = second_rows[:, at : at + 1] * 16.0 + second_rows[:, at + 1 : at + 2]
    slots = slots.astype(jnp.int32)
    lanes = lax.broadcasted_iota(jnp.int32, (per_owner, piece), 1)
    totals = []
    for outer in range(outers):
        base = (outer ^ my_outer) * piece
        totals.append(matmul(rows_down, one_hot(lanes == slots - base)).astype(jnp.bfloat16))
    for index in range(len(keep_refs)):

        @pl.when(place // 2 == first + index)
        def _(index=index):
            for outer in range(outers):
                ref = (send_refs if outer % 2 else keep_refs)[index]
                ref[0, outer // 2] = totals[outer]


def part_specs(start, first, count, part):
    def spec(index):
        begin = start + 2 * (count - 1 - index)
        return pl.BlockSpec(
            (1,) + part[1:], lambda i, *_: (jnp.clip(begin + 1 - i, 0, 1), 0, 0, 0)
        )

    return [spec(index) for index in range(count)] * 2


def local_grads(x_down, g_down, mix, lift_down, linear, ids, home, owners, part):
    samples, width, feats = x_down.shape
    rank = mix.shape[1]
    group = 16
    steps = samples // group
    per_owner = samples * feats // owners
    far_count = owners // 4
    shift = (part[1] * 2 * part[3]).bit_length() - 1
    sizes = (group, steps, owners, per_owner, 1.0 / math.sqrt(width), shift)

    def whole(shape):
        return pl.BlockSpec(shape, lambda i, *_: (0,) * len(shape))

    sample_spec = pl.BlockSpec(
        (group, width, feats), lambda i: (jnp.clip(i - 1, 0, steps - 1), 0, 0)
    )
    dense_rows = feats * (1 + feats // 128) + width
    outers = 2 * part[1]
    dense_piece = (dense_rows // outers, 128)
    room = per_owner + 64
    rows_shape = (owners // 2, per_owner, 256)
    scratch = [
        pltpu.VMEM((samples, feats), jnp.int32),
        pltpu.VMEM((samples, feats), jnp.int32),
        pltpu.VMEM((samples, 128), jnp.int32),
        pltpu.SMEM((samples, 128), jnp.int32),
        pltpu.SemaphoreType.DMA,
        pltpu.VMEM((rank, feats), jnp.bfloat16),
        pltpu.VMEM((rank, width), jnp.bfloat16),
        pltpu.VMEM((feats, rank), jnp.float32),
        pltpu.VMEM((width, rank), jnp.float32),
        pltpu.VMEM((feats, feats), jnp.float32),
        pltpu.VMEM((2, group, feats + 64, 128), jnp.float32),
        pltpu.VMEM((2, group, feats + 64, 128), jnp.float32),
        pltpu.VMEM((owners, room, 128), jnp.float32),
        pltpu.VMEM((owners, room, 128), jnp.float32),
        pltpu.VMEM((dense_rows, 128), jnp.float32),
        pltpu.SMEM((owners,), jnp.int32),
    ]
    outs = pl.pallas_call(
        functools.partial(grads_kernel, sizes),
        out_shape=[jax.ShapeDtypeStruct(part, jnp.bfloat16)] * (2 * far_count)
        + [
            jax.ShapeDtypeStruct(rows_shape, jnp.bfloat16),
        ]
        + [jax.ShapeDtypeStruct(dense_piece, jnp.float32)] * outers,
        grid=(1 + steps + owners // 2,),
        in_specs=[
            sample_spec,
            sample_spec,
            whole((feats, rank)),
            whole((width, rank)),
            whole((feats, feats)),
            whole((samples, feats)),
            whole(home.shape),
        ],
        out_specs=part_specs(1 + steps, owners // 2 - far_count, far_count, part)
        + [
            pl.BlockSpec(
                (1,) + rows_shape[1:],
                lambda i: (jnp.clip(i - 1 - steps, 0, owners // 2 - 1), 0, 0),
            )
        ]
        + [whole(dense_piece)] * outers,
        scratch_shapes=scratch,
        compiler_params=pltpu.CompilerParams(vmem_limit_bytes=60 * 2**20),
        cost_estimate=pl.CostEstimate(
            flops=2 * samples * feats * feats * 3072, bytes_accessed=12 * 2**20, transcendentals=0
        ),
        name="local_grads",
    )(x_down, g_down, mix, lift_down, linear, ids, home)
    keep, send = outs[:far_count], outs[far_count : 2 * far_count]
    return keep, send, outs[2 * far_count], outs[2 * far_count + 1 :]


def build_kernel(at, rows_ref, *refs):
    half = len(refs) // 2
    rows = rows_ref[0].astype(jnp.float32)
    place = 2 * half - 1 - pl.program_id(0)
    keep_refs, send_refs = refs[:half], refs[half:]
    outer, _ = positions()
    build_rows(at, outer, rows[:, :128], rows[:, 128:], place, 0, keep_refs, send_refs)


def build_parts(rows, part, width):
    places, per_owner, lanes = rows.shape
    far_count = places // 2
    outs = pl.pallas_call(
        functools.partial(build_kernel, width - 128),
        out_shape=[jax.ShapeDtypeStruct(part, jnp.bfloat16)] * places,
        grid=(places,),
        in_specs=[pl.BlockSpec((1, per_owner, lanes), lambda i: (places - 1 - i, 0, 0))],
        out_specs=part_specs(0, 0, far_count, part),
        compiler_params=pltpu.CompilerParams(vmem_limit_bytes=60 * 2**20),
        cost_estimate=pl.CostEstimate(
            flops=4 * part[3] * part[1] * part[0] * places * per_owner * lanes,
            bytes_accessed=6 * 2**20,
            transcendentals=0,
        ),
        name="build_parts",
    )(rows)
    return outs[:far_count], outs[far_count:]


def adagrad_kernel(me_ref, *refs):
    pieces, (table_ref, accum_ref) = refs[:2], refs[2:4]
    new_table_ref, new_accum_ref = refs[-2:]
    width = table_ref.shape[0]
    for index, piece in enumerate(pieces):

        @pl.when(pl.program_id(0) == index)
        def _(piece=piece):
            grad = piece[...].astype(jnp.float32)
            mean = jnp.sum(grad * grad, axis=0, keepdims=True) * (1.0 / width)
            updated = accum_ref[...] + mean
            new_accum_ref[...] = updated
            new_table_ref[...] = table_ref[...] - grad * (LEARN_RATE / jnp.sqrt(updated))


def update_table(me, pieces, table_down, accum, first, done=()):
    width, table_rows = table_down.shape
    piece = pieces[0].shape[1]

    def moved(rows):
        return pl.BlockSpec((rows, piece), lambda i, me: (0, (first + i) ^ me[0]))

    return pl.pallas_call(
        adagrad_kernel,
        out_shape=(
            jax.ShapeDtypeStruct((width, table_rows), jnp.float32),
            jax.ShapeDtypeStruct((1, table_rows), jnp.float32),
        ),
        grid_spec=pltpu.PrefetchScalarGridSpec(
            num_scalar_prefetch=1,
            grid=(2,),
            in_specs=[pl.BlockSpec(memory_space=pltpu.VMEM)] * 2
            + [moved(width), moved(1)]
            + [pl.BlockSpec(memory_space=pl.ANY)] * len(done),
            out_specs=[moved(width), moved(1)],
        ),
        input_output_aliases={5 + i: i for i in range(len(done))},
        compiler_params=pltpu.CompilerParams(vmem_limit_bytes=16 * 2**20),
        name="update_table",
    )(me, *pieces, table_down, accum, *done)


def swap(values, axis, bit):
    size = lax.axis_size(axis)
    return lax.ppermute(values, axis, [(i, i ^ bit) for i in range(size)])


def add_half(first, second):
    return (first.astype(jnp.float32) + second.astype(jnp.float32)).astype(jnp.bfloat16)


def tree_sum(values):
    while len(values) > 1:
        values = [values[i] + values[i + 1] for i in range(0, len(values), 2)]
    return values[0]


def after(value, *ready):
    return lax.optimization_barrier((value,) + ready)[0]


def halves(dense, side):
    cut = dense.reshape(2, dense.shape[0] // 2, dense.shape[1])
    mine = lax.dynamic_index_in_dim(cut, side, 0, keepdims=False)
    return mine, lax.dynamic_index_in_dim(cut, 1 - side, 0, keepdims=False)


def stacked(dense, other, side):
    return jnp.where(side == 0, jnp.stack([dense, other]), jnp.stack([other, dense]))


def sum_all(me, keep, send, rows, dense, part, width):
    owners = lax.axis_size("inner")
    outer, inner = lax.axis_index("outer"), lax.axis_index("inner")
    far_count = owners // 2
    first = far_count - len(keep)
    keep = dict(enumerate(keep, first))
    came, parts, kept, sent, rest, second, terms, last = ({} for _ in range(8))
    far_ones, near_ones = list(reversed(range(first, far_count))), list(reversed(range(first)))

    def first_stage(far):
        held = keep[far]
        if far % 2:
            parts[far] = add_half(held[1], came[far][1])
            kept[far] = add_half(held[0], came[far][0])
        else:
            parts[far] = add_half(held[:, 1], came[far][:, 1])
            kept[far] = add_half(held[:, 0], came[far][:, 0])

    def second_stage(far):
        parts[far] = add_half(kept[far][1], sent[far][1])
        rest[far] = add_half(kept[far][0], sent[far][0])
        second[far] = swap(parts[far], *(("outer", 2) if far % 2 else ("inner", 1)))

    def send_first(far, ready):
        sent[far] = swap(ready, *(("inner", 1) if far % 2 else ("outer", 2)))

    sides = (outer & 1, outer >> 1, inner & 1)
    for far in far_ones:
        came[far] = swap(send[far - first], "outer", 1)
    others = tuple(swap(dense[bits], "outer", bits) for bits in range(1, len(dense)))
    for far in far_ones:
        first_stage(far)
        send_first(far, parts[far])
    far_parts = [parts[far] for far in far_ones]
    rows = after(rows, *far_parts)
    low_keep, low_send = build_parts(rows, part, width)
    for far in near_ones:
        keep[far] = low_keep[far]
        came[far] = swap(low_send[far], "outer", 1)
    dense = sum_list((dense[0],) + after(others, low_send[0]))
    mine, other = halves(dense, sides[2])
    other = swap(other, "inner", 1)
    for far in far_ones:
        second_stage(far)
    for far in near_ones:
        first_stage(far)
    near_parts = [parts[far] for far in near_ones]
    for far in near_ones:
        send_first(far, parts[far])
    dense = mine + after(other, *near_parts)
    other = swap(dense, "inner", 2)

    def send_last(far, *ready):
        low = far & -far
        value = rest[far].astype(jnp.float32) + second[far].astype(jnp.float32)
        came_far = [terms[far + bit] for bit in (1 << at for at in range(8)) if bit < low]
        if came_far:
            for one in after(tuple(came_far), *ready):
                value = value + one.astype(jnp.float32)
        last[far] = value.astype(jnp.bfloat16)
        terms[far] = swap(last[far], "inner", 2 * low)

    for far in far_ones:
        second[far] = after(second[far], me, dense, *near_parts)
    odd_ones = [far for far in far_ones if far % 2]
    for far in odd_ones:
        send_last(far)
    odd_last = [last[far] for far in odd_ones]
    for bit in range(1, far_count.bit_length() - 1):
        dense = dense + after(other, *odd_last)
        other = swap(dense, "inner", 2 << bit)
    arrived = after(tuple(sent[far] for far in near_ones), *odd_last)
    for far, sent[far] in zip(near_ones, arrived):
        second_stage(far)
    near_parts = [parts[far] for far in near_ones]
    dense = dense + after(other, *near_parts)
    other = swap(dense, "inner", 1)
    for far in far_ones:
        if far % 2 == 0:
            send_last(far, *near_parts)
    even_last = [last[far] for far in far_ones if far % 2 == 0]
    for far in near_ones:
        second[far] = after(second[far], *even_last)
        if far:
            send_last(far)
    dense = stacked(dense, after(other, last[1]), sides[2])
    other = swap(dense, "outer", 2)
    dense = stacked(dense, after(other, second[0], terms[2]), sides[1])
    mine, came_last = after((rest[0], second[0]), dense, last[1])
    total = mine.astype(jnp.float32) + came_last.astype(jnp.float32)
    ends = tuple(terms[1 << bit] for bit in range(far_count.bit_length() - 1))
    for term in after(ends, dense, last[1]):
        total = total + term.astype(jnp.float32)
    total = total.astype(jnp.bfloat16)
    across = swap(total, "outer", 2)
    beside = swap(total, "outer", 1)
    dense = stacked(dense, swap(dense, "outer", 1), sides[0])
    lanes = dense.shape[-1]
    return total, beside, across, jnp.transpose(dense, (1, 0, 2, 3, 4)).reshape(-1, lanes)


def dense_table(
    layer_input,
    out_grad,
    mix_weight,
    lift_weight,
    linear_weight,
    row_ids,
    row_home,
    table,
    row_accum,
):
    owners, outers = lax.axis_size("inner"), lax.axis_size("outer")
    sample_count = layer_input.shape[0]
    table_rows = table.shape[0]
    me = jnp.stack([lax.axis_index("outer"), lax.axis_index("inner")]).astype(jnp.int32)
    width = layer_input.shape[2]
    part = (2, outers // 2, width, table_rows // outers)
    keep, send, rows, dense = local_grads(
        jnp.swapaxes(layer_input, 1, 2),
        jnp.swapaxes(out_grad, 1, 2),
        mix_weight,
        lift_weight.T,
        linear_weight,
        row_ids,
        row_home.reshape(-1, 128),
        owners,
        part,
    )
    total, beside, across, dense = sum_all(me, keep, send, rows, dense, part, width)
    dense = dense * (1.0 / (sample_count * outers * owners))
    feats = layer_input.shape[1]
    linear = [dense[feats * (1 + i) : feats * (2 + i)] for i in range(feats // 128)]
    weights = (
        dense[:feats],
        dense[feats * (1 + feats // 128) :].T,
        jnp.concatenate(linear, axis=1),
    )
    table_down, accum = table.T, row_accum.reshape(1, -1)
    done = update_table(me, (total, beside), table_down, accum, 0)
    across = after(across, done[1], *weights)
    pieces = (across, swap(across, "outer", 1))
    new_table, new_accum = update_table(me, pieces, table_down, accum, 2, done)
    return (new_table.T, new_accum.reshape(-1)) + weights


def power_of_two(number):
    return number & (number - 1) == 0


def on_device(*arrays):
    owners, outers = lax.axis_size("inner"), lax.axis_size("outer")
    layer_input, mix_weight, row_home, table = (arrays[i] for i in (0, 2, 6, 7))
    samples, feats, width = layer_input.shape
    dense_fits = (
        outers == 4
        and owners % 4 == 0
        and power_of_two(owners)
        and row_home.shape[0] <= 2 * samples * feats
        and row_home.shape[0] <= 2**15
        and power_of_two(table.shape[0])
        and 512 <= table.shape[0] <= 4096
        and samples % 16 == 0
        and (feats * (1 + feats // 128) + width) % 64 == 0
        and feats == 256
        and mix_weight.shape[1] == 128
        and 2 * (width - 128) == 128
    )
    return dense_table(*arrays) if dense_fits else routed_rows(*arrays)


def solution(mesh):
    placed = (
        P(("outer", "inner"), None, None),
        P(("outer", "inner"), None, None),
        P(),
        P(),
        P(),
        P(("outer", "inner"), None),
        P(),
        P("inner", None),
        P("inner"),
    )
    return jax.shard_map(
        on_device,
        mesh=mesh,
        in_specs=placed,
        out_specs=(P("inner", None), P("inner"), P(), P(), P()),
        check_vma=False,
    )
```

profile of v0, /device:TPU:0, one launch (start us, length us, event | category | flops | bytes accessed | tf_op | source)
XLA Modules:
  0.0 86.9 jit_solution(17322247568122454585)
XLA Ops:
  0.6 26.3 %local_grads.1 = (bf16[2,2,192,512]{3,2,1,0:T(8,128)(2,1)}, bf16[2,2,192,512]{3,2,1,0:T(8,128)(2,1)}, bf16[2,2,192,512]{3,2,1,0:T(8,128)(2,1)}, bf16[2,2,192,512...) custom-call(bf16[32,192,256]{2,1,0:T(8,128)(2,1)} %bitcast.129, ...), custom_call_target="tpu_custom_call" | custom-call | flops 12884901888 | bytes 12582912 | tf_op jit(solution)/shard_map/local_grads/pallas_call | solution.py:486
  27.5 2.7 %collective-permute-start.10 = (f32[240,128]{1,0:T(8,128)}, f32[240,128]{1,0:T(8,128)S(1)}, u32[]{:S(2)}, u32[]{:S(2)}) collective-permute-start(f32[240,128]{1,0:T(8,128)} %get-tuple-element.56), channel_id=1, source_target_pairs={{0,24},{8,16},{16,8},{24,0},{1,25},{9,17},{17,9},{25,1},{2,26},{10... | collective-permute-start | bytes 368648 | tf_op jit(solution)/shard_map/ppermute | solution.py:595
  30.7 1.3 %add_convert_fusion.2 = (bf16[1,2,192,512]{3,2,1,0:T(8,128)(2,1)S(1)}, bf16[2,192,512]{2,1,0:T(8,128)(2,1)S(1)}) fusion(bf16[2,2,192,512]{3,2,1,0:T(8,128)(2,1)S(1)} %collective-permute-done, bf16[2,2,192,512]{3,2,1,0:T(8,128)(2,1)} %get-tuple-element.44), kind=kLoop, calls=%fused_computation.2 | loop fusion | flops 1572864 | bytes 2359296 | tf_op jit(solution)/shard_map/convert_element_type | solution.py:599
  32.0 2.0 %collective-permute-start.6 = (bf16[2,192,512]{2,1,0:T(8,128)(2,1)S(1)}, bf16[2,192,512]{2,1,0:T(8,128)(2,1)S(1)}, u32[]{:S(2)}, u32[]{:S(2)}) collective-permute-start(bf16[2,192,512]{2,1,0:T(8,128)(2,1)S(1)} %get-tuple-element.86), channel_id=1, source_target_pairs={{0,1},{1,0},{2,3},{3,2},{4,5},{5,4},{6,7},{7,6},{8,9},{9,8},{10,11... | collective-permute-start | bytes 1179656 | tf_op jit(solution)/shard_map/ppermute | solution.py:595
  34.3 1.6 %collective-permute-start.13 = (bf16[2,192,512]{2,1,0:T(8,128)(2,1)S(1)}, bf16[2,192,512]{2,1,0:T(8,128)(2,1)S(1)}, u32[]{:S(2)}, u32[]{:S(2)}) collective-permute-start(bf16[2,192,512]{2,1,0:T(8,128)(2,1)S(1)} %get-tuple-element.82), channel_id=1, source_target_pairs={{0,16},{8,24},{16,0},{24,8},{1,17},{9,25},{17,1},{25,9},{2,18},{10... | collective-permute-start | bytes 1179656 | tf_op jit(solution)/shard_map/ppermute | solution.py:595
  35.9 8.0 %build_parts.1 = (bf16[2,2,192,512]{3,2,1,0:T(8,128)(2,1)}, bf16[2,2,192,512]{3,2,1,0:T(8,128)(2,1)}, bf16[2,2,192,512]{3,2,1,0:T(8,128)(2,1)}, bf16[2,2,192,512]{3,2,1,0:T(8,128)(2,1)}) custom-call(bf16[4,1024,256]{2,1,0:T(8,128)(2,1)} %get-tuple-element.48.rows_ref), custom_call_target="tpu_custom_call" | custom-call | flops 8589934592 | bytes 6291456 | tf_op jit(solution)/shard_map/build_parts/pallas_call | solution.py:534
  45.5 2.0 %collective-permute-start.14 = (bf16[192,512]{1,0:T(8,128)(2,1)S(1)}, bf16[192,512]{1,0:T(8,128)(2,1)S(1)}, u32[]{:S(2)}, u32[]{:S(2)}) collective-permute-start(bf16[192,512]{1,0:T(8,128)(2,1)S(1)} %fusion.23), channel_id=1, source_target_pairs={{0,1},{1,0},{2,3},{3,2},{4,5},{5,4},{6,7},{7,6},{8,9},{9,8},{10,11... | collective-permute-start | bytes 589832 | tf_op jit(solution)/shard_map/ppermute | solution.py:595
  47.7 1.6 %collective-permute-start.5 = (bf16[2,192,512]{2,1,0:T(8,128)(2,1)S(1)}, bf16[2,192,512]{2,1,0:T(8,128)(2,1)S(1)}, u32[]{:S(2)}, u32[]{:S(2)}) collective-permute-start(bf16[2,192,512]{2,1,0:T(8,128)(2,1)S(1)} %get-tuple-element.84), channel_id=1, source_target_pairs={{0,16},{8,24},{16,0},{24,8},{1,17},{9,25},{17,1},{25,9},{2,18},{10... | collective-permute-start | bytes 1179656 | tf_op jit(solution)/shard_map/ppermute | solution.py:595
  50.1 1.6 %collective-permute-start.16 = (f32[120,128]{1,0:T(8,128)S(1)}, f32[120,128]{1,0:T(8,128)S(1)}, u32[]{:S(2)}, u32[]{:S(2)}) collective-permute-start(f32[120,128]{1,0:T(8,128)S(1)} %bitcast_add_fusion), channel_id=1, source_target_pairs={{0,2},{1,3},{2,0},{3,1},{4,6},{5,7},{6,4},{7,5},{8,10},{9,11},{10,... | collective-permute-start | bytes 184328 | tf_op jit(solution)/shard_map/ppermute | solution.py:595
  51.8 1.4 %collective-permute-done.7 = bf16[192,512]{1,0:T(8,128)(2,1)S(1)} collective-permute-done((bf16[192,512]{1,0:T(8,128)(2,1)S(1)}, bf16[192,512]{1,0:T(8,128)(2,1)S(1)}, u32[]{:S(2)}, u32[]{:S(2)}) %collective-permute-start.7) | collective-permute-done | bytes 196640 | tf_op jit(solution)/shard_map/ppermute | solution.py:595
  53.8 1.6 %collective-permute-start.15 = (bf16[192,512]{1,0:T(8,128)(2,1)S(1)}, bf16[192,512]{1,0:T(8,128)(2,1)S(1)}, u32[]{:S(2)}, u32[]{:S(2)}) collective-permute-start(bf16[192,512]{1,0:T(8,128)(2,1)S(1)} %fusion.14), channel_id=1, source_target_pairs={{0,2},{1,3},{2,0},{3,1},{4,6},{5,7},{6,4},{7,5},{8,10},{9,11},{10,... | collective-permute-start | bytes 589832 | tf_op jit(solution)/shard_map/ppermute | solution.py:595
  55.4 2.7 %collective-permute-start.17 = (f32[120,128]{1,0:T(8,128)S(1)}, f32[120,128]{1,0:T(8,128)S(1)}, u32[]{:S(2)}, u32[]{:S(2)}) collective-permute-start(f32[120,128]{1,0:T(8,128)S(1)} %add.135), channel_id=1, source_target_pairs={{0,4},{1,5},{2,6},{3,7},{4,0},{5,1},{6,2},{7,3},{8,12},{9,13},{10,... | collective-permute-start | bytes 184328 | tf_op jit(solution)/shard_map/ppermute | solution.py:595
  58.0 2.4 %collective-permute-done.5 = bf16[2,192,512]{2,1,0:T(8,128)(2,1)S(1)} collective-permute-done((bf16[2,192,512]{2,1,0:T(8,128)(2,1)S(1)}, bf16[2,192,512]{2,1,0:T(8,128)(2,1)S(1)}, u32[]{:S(2)}, u32[]{:S(2)}) %collective-permute-start.5) | collective-permute-done | bytes 393248 | tf_op jit(solution)/shard_map/ppermute | solution.py:595
  60.4 1.1 %collective-permute-done.4 = bf16[2,192,512]{2,1,0:T(8,128)(2,1)S(1)} collective-permute-done((bf16[2,192,512]{2,1,0:T(8,128)(2,1)S(1)}, bf16[2,192,512]{2,1,0:T(8,128)(2,1)S(1)}, u32[]{:S(2)}, u32[]{:S(2)}) %collective-permute-start.4) | collective-permute-done | bytes 393248 | tf_op jit(solution)/shard_map/ppermute | solution.py:595
  62.6 1.8 %collective-permute-start.12 = (bf16[192,512]{1,0:T(8,128)(2,1)S(1)}, bf16[192,512]{1,0:T(8,128)(2,1)S(1)}, u32[]{:S(2)}, u32[]{:S(2)}) collective-permute-start(bf16[192,512]{1,0:T(8,128)(2,1)S(1)} %get-tuple-element.90), channel_id=1, source_target_pairs={{0,1},{1,0},{2,3},{3,2},{4,5},{5,4},{6,7},{7,6},{8,9},{9,8},{10,11... | collective-permute-start | bytes 589832 | tf_op jit(solution)/shard_map/ppermute | solution.py:595
  64.9 2.6 %collective-permute-start.21 = (bf16[192,512]{1,0:T(8,128)(2,1)S(1)}, bf16[192,512]{1,0:T(8,128)(2,1)S(1)}, u32[]{:S(2)}, u32[]{:S(2)}) collective-permute-start(bf16[192,512]{1,0:T(8,128)(2,1)S(1)} %fusion.10), channel_id=1, source_target_pairs={{0,4},{1,5},{2,6},{3,7},{4,0},{5,1},{6,2},{7,3},{8,12},{9,13},{10,... | collective-permute-start | bytes 589832 | tf_op jit(solution)/shard_map/ppermute | solution.py:595
  67.8 1.6 %collective-permute-start.22 = (bf16[192,512]{1,0:T(8,128)(2,1)S(1)}, bf16[192,512]{1,0:T(8,128)(2,1)S(1)}, u32[]{:S(2)}, u32[]{:S(2)}) collective-permute-start(bf16[192,512]{1,0:T(8,128)(2,1)S(1)} %fusion.5), channel_id=1, source_target_pairs={{0,2},{1,3},{2,0},{3,1},{4,6},{5,7},{6,4},{7,5},{8,10},{9,11},{10,... | collective-permute-start | bytes 589832 | tf_op jit(solution)/shard_map/ppermute | solution.py:595
  69.5 1.6 %collective-permute-start.20 = (f32[2,120,128]{2,1,0:T(8,128)S(1)}, f32[2,120,128]{2,1,0:T(8,128)S(1)}, u32[]{:S(2)}, u32[]{:S(2)}) collective-permute-start(f32[2,120,128]{2,1,0:T(8,128)S(1)} %maximum_select_fusion.3), channel_id=1, source_target_pairs={{0,16},{8,24},{16,0},{24,8},{1,17},{9,25},{17,1},{25,9},{2,18},{10... | collective-permute-start | bytes 368648 | tf_op jit(solution)/shard_map/ppermute | solution.py:595
  71.1 4.0 %collective-permute-done.21 = bf16[192,512]{1,0:T(8,128)(2,1)S(1)} collective-permute-done((bf16[192,512]{1,0:T(8,128)(2,1)S(1)}, bf16[192,512]{1,0:T(8,128)(2,1)S(1)}, u32[]{:S(2)}, u32[]{:S(2)}) %collective-permute-start.21) | collective-permute-done | bytes 196640 | tf_op jit(solution)/shard_map/ppermute | solution.py:595
  75.3 1.0 %collective-permute-done.22 = bf16[192,512]{1,0:T(8,128)(2,1)S(1)} collective-permute-done((bf16[192,512]{1,0:T(8,128)(2,1)S(1)}, bf16[192,512]{1,0:T(8,128)(2,1)S(1)}, u32[]{:S(2)}, u32[]{:S(2)}) %collective-permute-start.22) | collective-permute-done | bytes 196640 | tf_op jit(solution)/shard_map/ppermute | solution.py:595
  79.5 1.7 %update_table.2 = (f32[192,2048]{1,0:T(8,128)}, f32[1,2048]{1,0:T(1,128)}) custom-call(s32[2]{0:T(128)S(1)} %pad_add_fusion.me_ref, bf16[192,512]{1,0:T(8,128)(2,1)S(1)} %add_convert_fusion.8.refs_0_, bf16[192,512]{1,0:T(8,128)(2,1)S(1)} %collective-permute-done.24.refs_1_, f32[192,2048]{1,0:T(8,128)S(1)} %bitcast.110, f32[1,2048]{1,0:T(1,128)S(1)} %bitcast.112), custom_call_target="tpu_custom_call" | custom-call | tf_op jit(solution)/shard_map/update_table/pallas_call | solution.py:573
  81.2 2.6 %collective-permute-done.23.refs_0_ = bf16[192,512]{1,0:T(8,128)(2,1)S(1)} collective-permute-done((bf16[192,512]{1,0:T(8,128)(2,1)S(1)}, bf16[192,512]{1,0:T(8,128)(2,1)S(1)}, u32[]{:S(2)}, u32[]{:S(2)}) %collective-permute-start.23) | collective-permute-done | bytes 196640 | tf_op jit(solution)/shard_map/ppermute | solution.py:595
  83.8 1.4 %collective-permute-done.26.refs_1_ = bf16[192,512]{1,0:T(8,128)(2,1)S(1)} collective-permute-done((bf16[192,512]{1,0:T(8,128)(2,1)S(1)}, bf16[192,512]{1,0:T(8,128)(2,1)S(1)}, u32[]{:S(2)}, u32[]{:S(2)}) %collective-permute-start.26) | collective-permute-done | bytes 196640 | tf_op jit(solution)/shard_map/ppermute | solution.py:595
  85.2 1.7 %update_table.3 = (f32[192,2048]{1,0:T(8,128)}, f32[1,2048]{1,0:T(1,128)}) custom-call(s32[2]{0:T(128)S(1)} %pad_add_fusion.me_ref, bf16[192,512]{1,0:T(8,128)(2,1)S(1)} %collective-permute-done.23.refs_0_, bf16[192,512]{1,0:T(8,128)(2,1)S(1)} %collective-permute-done.26.refs_1_, ...), custom_call_target="tpu_custom_call", output_to_operand_aliasing={{0}: (5, {}), {1}: (6, {})} | custom-call | tf_op jit(solution)/shard_map/update_table/pallas_call | solution.py:573
  (73 shorter events, 9.7 us)
Async XLA Ops:
  26.9 3.8 %collective-permute-start = (bf16[2,2,192,512]{3,2,1,0:T(8,128)(2,1)}, bf16[2,2,192,512]{3,2,1,0:T(8,128)(2,1)S(1)}, u32[]{:S(2)}, u32[]{:S(2)}) collective-permute-start(bf16[2,2,192,512]{3,2,1,0:T(8,128)(2,1)} %get-tuple-element.45), channel_id=1, source_target_pairs={{0,8},{8,0},{16,24},{24,16},{1,9},{9,1},{17,25},{25,17},{2,10},{10... | collective-permute-start | bytes 2359304 | tf_op jit(solution)/shard_map/ppermute | solution.py:595
  27.4 6.6 %collective-permute-start.1 = (bf16[2,2,192,512]{3,2,1,0:T(8,128)(2,1)}, bf16[2,2,192,512]{3,2,1,0:T(8,128)(2,1)S(1)}, u32[]{:S(2)}, u32[]{:S(2)}) collective-permute-start(bf16[2,2,192,512]{3,2,1,0:T(8,128)(2,1)} %get-tuple-element.47), channel_id=1, source_target_pairs={{0,8},{8,0},{16,24},{24,16},{1,9},{9,1},{17,25},{25,17},{2,10},{10... | collective-permute-start | bytes 2359304 | tf_op jit(solution)/shard_map/ppermute | solution.py:595
  27.5 16.5 %collective-permute-start.10 = (f32[240,128]{1,0:T(8,128)}, f32[240,128]{1,0:T(8,128)S(1)}, u32[]{:S(2)}, u32[]{:S(2)}) collective-permute-start(f32[240,128]{1,0:T(8,128)} %get-tuple-element.56), channel_id=1, source_target_pairs={{0,24},{8,16},{16,8},{24,0},{1,25},{9,17},{17,9},{25,1},{2,26},{10... | collective-permute-start | bytes 368648 | tf_op jit(solution)/shard_map/ppermute | solution.py:595
  30.2 13.9 %collective-permute-start.8 = (f32[240,128]{1,0:T(8,128)}, f32[240,128]{1,0:T(8,128)S(1)}, u32[]{:S(2)}, u32[]{:S(2)}) collective-permute-start(f32[240,128]{1,0:T(8,128)} %get-tuple-element.54), channel_id=1, source_target_pairs={{0,8},{8,0},{16,24},{24,16},{1,9},{9,1},{17,25},{25,17},{2,10},{10... | collective-permute-start | bytes 368648 | tf_op jit(solution)/shard_map/ppermute | solution.py:595
  30.6 13.5 %collective-permute-start.9 = (f32[240,128]{1,0:T(8,128)}, f32[240,128]{1,0:T(8,128)S(1)}, u32[]{:S(2)}, u32[]{:S(2)}) collective-permute-start(f32[240,128]{1,0:T(8,128)} %get-tuple-element.55), channel_id=1, source_target_pairs={{0,16},{8,24},{16,0},{24,8},{1,17},{9,25},{17,1},{25,9},{2,18},{10... | collective-permute-start | bytes 368648 | tf_op jit(solution)/shard_map/ppermute | solution.py:595
  32.0 13.2 %collective-permute-start.6 = (bf16[2,192,512]{2,1,0:T(8,128)(2,1)S(1)}, bf16[2,192,512]{2,1,0:T(8,128)(2,1)S(1)}, u32[]{:S(2)}, u32[]{:S(2)}) collective-permute-start(bf16[2,192,512]{2,1,0:T(8,128)(2,1)S(1)} %get-tuple-element.86), channel_id=1, source_target_pairs={{0,1},{1,0},{2,3},{3,2},{4,5},{5,4},{6,7},{7,6},{8,9},{9,8},{10,11... | collective-permute-start | bytes 1179656 | tf_op jit(solution)/shard_map/ppermute | solution.py:595
  34.3 11.1 %collective-permute-start.13 = (bf16[2,192,512]{2,1,0:T(8,128)(2,1)S(1)}, bf16[2,192,512]{2,1,0:T(8,128)(2,1)S(1)}, u32[]{:S(2)}, u32[]{:S(2)}) collective-permute-start(bf16[2,192,512]{2,1,0:T(8,128)(2,1)S(1)} %get-tuple-element.82), channel_id=1, source_target_pairs={{0,16},{8,24},{16,0},{24,8},{1,17},{9,25},{17,1},{25,9},{2,18},{10... | collective-permute-start | bytes 1179656 | tf_op jit(solution)/shard_map/ppermute | solution.py:595
  44.0 3.5 %collective-permute-start.2 = (bf16[2,2,192,512]{3,2,1,0:T(8,128)(2,1)}, bf16[2,2,192,512]{3,2,1,0:T(8,128)(2,1)S(1)}, u32[]{:S(2)}, u32[]{:S(2)}) collective-permute-start(bf16[2,2,192,512]{3,2,1,0:T(8,128)(2,1)} %get-tuple-element.50), channel_id=1, source_target_pairs={{0,8},{8,0},{16,24},{24,16},{1,9},{9,1},{17,25},{25,17},{2,10},{10... | collective-permute-start | bytes 2359304 | tf_op jit(solution)/shard_map/ppermute | solution.py:595
  44.1 5.2 %collective-permute-start.3 = (bf16[2,2,192,512]{3,2,1,0:T(8,128)(2,1)}, bf16[2,2,192,512]{3,2,1,0:T(8,128)(2,1)S(1)}, u32[]{:S(2)}, u32[]{:S(2)}) collective-permute-start(bf16[2,2,192,512]{3,2,1,0:T(8,128)(2,1)} %get-tuple-element.52), channel_id=1, source_target_pairs={{0,8},{8,0},{16,24},{24,16},{1,9},{9,1},{17,25},{25,17},{2,10},{10... | collective-permute-start | bytes 2359304 | tf_op jit(solution)/shard_map/ppermute | solution.py:595
  44.6 5.5 %collective-permute-start.11 = (f32[120,128]{1,0:T(8,128)S(1)}, f32[120,128]{1,0:T(8,128)S(1)}, u32[]{:S(2)}, u32[]{:S(2)}) collective-permute-start(f32[120,128]{1,0:T(8,128)S(1)} %dynamic-slice_bitcast_fusion), channel_id=1, source_target_pairs={{0,1},{1,0},{2,3},{3,2},{4,5},{5,4},{6,7},{7,6},{8,9},{9,8},{10,11... | collective-permute-start | bytes 184328 | tf_op jit(solution)/shard_map/ppermute | solution.py:595
  45.3 7.9 %collective-permute-start.7 = (bf16[192,512]{1,0:T(8,128)(2,1)S(1)}, bf16[192,512]{1,0:T(8,128)(2,1)S(1)}, u32[]{:S(2)}, u32[]{:S(2)}) collective-permute-start(bf16[192,512]{1,0:T(8,128)(2,1)S(1)} %fusion.20), channel_id=1, source_target_pairs={{0,16},{8,24},{16,0},{24,8},{1,17},{9,25},{17,1},{25,9},{2,18},{10... | collective-permute-start | bytes 589832 | tf_op jit(solution)/shard_map/ppermute | solution.py:595
  45.5 8.3 %collective-permute-start.14 = (bf16[192,512]{1,0:T(8,128)(2,1)S(1)}, bf16[192,512]{1,0:T(8,128)(2,1)S(1)}, u32[]{:S(2)}, u32[]{:S(2)}) collective-permute-start(bf16[192,512]{1,0:T(8,128)(2,1)S(1)} %fusion.23), channel_id=1, source_target_pairs={{0,1},{1,0},{2,3},{3,2},{4,5},{5,4},{6,7},{7,6},{8,9},{9,8},{10,11... | collective-permute-start | bytes 589832 | tf_op jit(solution)/shard_map/ppermute | solution.py:595
  47.7 12.7 %collective-permute-start.5 = (bf16[2,192,512]{2,1,0:T(8,128)(2,1)S(1)}, bf16[2,192,512]{2,1,0:T(8,128)(2,1)S(1)}, u32[]{:S(2)}, u32[]{:S(2)}) collective-permute-start(bf16[2,192,512]{2,1,0:T(8,128)(2,1)S(1)} %get-tuple-element.84), channel_id=1, source_target_pairs={{0,16},{8,24},{16,0},{24,8},{1,17},{9,25},{17,1},{25,9},{2,18},{10... | collective-permute-start | bytes 1179656 | tf_op jit(solution)/shard_map/ppermute | solution.py:595
  49.5 11.9 %collective-permute-start.4 = (bf16[2,192,512]{2,1,0:T(8,128)(2,1)S(1)}, bf16[2,192,512]{2,1,0:T(8,128)(2,1)S(1)}, u32[]{:S(2)}, u32[]{:S(2)}) collective-permute-start(bf16[2,192,512]{2,1,0:T(8,128)(2,1)S(1)} %get-tuple-element.87), channel_id=1, source_target_pairs={{0,1},{1,0},{2,3},{3,2},{4,5},{5,4},{6,7},{7,6},{8,9},{9,8},{10,11... | collective-permute-start | bytes 1179656 | tf_op jit(solution)/shard_map/ppermute | solution.py:595
  50.1 5.2 %collective-permute-start.16 = (f32[120,128]{1,0:T(8,128)S(1)}, f32[120,128]{1,0:T(8,128)S(1)}, u32[]{:S(2)}, u32[]{:S(2)}) collective-permute-start(f32[120,128]{1,0:T(8,128)S(1)} %bitcast_add_fusion), channel_id=1, source_target_pairs={{0,2},{1,3},{2,0},{3,1},{4,6},{5,7},{6,4},{7,5},{8,10},{9,11},{10,... | collective-permute-start | bytes 184328 | tf_op jit(solution)/shard_map/ppermute | solution.py:595
  53.8 11.0 %collective-permute-start.15 = (bf16[192,512]{1,0:T(8,128)(2,1)S(1)}, bf16[192,512]{1,0:T(8,128)(2,1)S(1)}, u32[]{:S(2)}, u32[]{:S(2)}) collective-permute-start(bf16[192,512]{1,0:T(8,128)(2,1)S(1)} %fusion.14), channel_id=1, source_target_pairs={{0,2},{1,3},{2,0},{3,1},{4,6},{5,7},{6,4},{7,5},{8,10},{9,11},{10,... | collective-permute-start | bytes 589832 | tf_op jit(solution)/shard_map/ppermute | solution.py:595
  55.4 9.0 %collective-permute-start.17 = (f32[120,128]{1,0:T(8,128)S(1)}, f32[120,128]{1,0:T(8,128)S(1)}, u32[]{:S(2)}, u32[]{:S(2)}) collective-permute-start(f32[120,128]{1,0:T(8,128)S(1)} %add.135), channel_id=1, source_target_pairs={{0,4},{1,5},{2,6},{3,7},{4,0},{5,1},{6,2},{7,3},{8,12},{9,13},{10,... | collective-permute-start | bytes 184328 | tf_op jit(solution)/shard_map/ppermute | solution.py:595
  61.5 6.2 %collective-permute-start.19 = (bf16[192,512]{1,0:T(8,128)(2,1)S(1)}, bf16[192,512]{1,0:T(8,128)(2,1)S(1)}, u32[]{:S(2)}, u32[]{:S(2)}) collective-permute-start(bf16[192,512]{1,0:T(8,128)(2,1)S(1)} %fusion.24), channel_id=1, source_target_pairs={{0,16},{8,24},{16,0},{24,8},{1,17},{9,25},{17,1},{25,9},{2,18},{10... | collective-permute-start | bytes 589832 | tf_op jit(solution)/shard_map/ppermute | solution.py:595
  62.6 8.5 %collective-permute-start.12 = (bf16[192,512]{1,0:T(8,128)(2,1)S(1)}, bf16[192,512]{1,0:T(8,128)(2,1)S(1)}, u32[]{:S(2)}, u32[]{:S(2)}) collective-permute-start(bf16[192,512]{1,0:T(8,128)(2,1)S(1)} %get-tuple-element.90), channel_id=1, source_target_pairs={{0,1},{1,0},{2,3},{3,2},{4,5},{5,4},{6,7},{7,6},{8,9},{9,8},{10,11... | collective-permute-start | bytes 589832 | tf_op jit(solution)/shard_map/ppermute | solution.py:595
  64.4 5.1 %collective-permute-start.18 = (f32[120,128]{1,0:T(8,128)S(1)}, f32[120,128]{1,0:T(8,128)S(1)}, u32[]{:S(2)}, u32[]{:S(2)}) collective-permute-start(f32[120,128]{1,0:T(8,128)S(1)} %add.136), channel_id=1, source_target_pairs={{0,1},{1,0},{2,3},{3,2},{4,5},{5,4},{6,7},{7,6},{8,9},{9,8},{10,11... | collective-permute-start | bytes 184328 | tf_op jit(solution)/shard_map/ppermute | solution.py:595
  64.9 10.3 %collective-permute-start.21 = (bf16[192,512]{1,0:T(8,128)(2,1)S(1)}, bf16[192,512]{1,0:T(8,128)(2,1)S(1)}, u32[]{:S(2)}, u32[]{:S(2)}) collective-permute-start(bf16[192,512]{1,0:T(8,128)(2,1)S(1)} %fusion.10), channel_id=1, source_target_pairs={{0,4},{1,5},{2,6},{3,7},{4,0},{5,1},{6,2},{7,3},{8,12},{9,13},{10,... | collective-permute-start | bytes 589832 | tf_op jit(solution)/shard_map/ppermute | solution.py:595
  67.8 8.4 %collective-permute-start.22 = (bf16[192,512]{1,0:T(8,128)(2,1)S(1)}, bf16[192,512]{1,0:T(8,128)(2,1)S(1)}, u32[]{:S(2)}, u32[]{:S(2)}) collective-permute-start(bf16[192,512]{1,0:T(8,128)(2,1)S(1)} %fusion.5), channel_id=1, source_target_pairs={{0,2},{1,3},{2,0},{3,1},{4,6},{5,7},{6,4},{7,5},{8,10},{9,11},{10,... | collective-permute-start | bytes 589832 | tf_op jit(solution)/shard_map/ppermute | solution.py:595
  69.5 5.6 %collective-permute-start.20 = (f32[2,120,128]{2,1,0:T(8,128)S(1)}, f32[2,120,128]{2,1,0:T(8,128)S(1)}, u32[]{:S(2)}, u32[]{:S(2)}) collective-permute-start(f32[2,120,128]{2,1,0:T(8,128)S(1)} %maximum_select_fusion.3), channel_id=1, source_target_pairs={{0,16},{8,24},{16,0},{24,8},{1,17},{9,25},{17,1},{25,9},{2,18},{10... | collective-permute-start | bytes 368648 | tf_op jit(solution)/shard_map/ppermute | solution.py:595
  76.5 7.3 %collective-permute-start.23 = (bf16[192,512]{1,0:T(8,128)(2,1)S(1)}, bf16[192,512]{1,0:T(8,128)(2,1)S(1)}, u32[]{:S(2)}, u32[]{:S(2)}) collective-permute-start(bf16[192,512]{1,0:T(8,128)(2,1)S(1)} %add_convert_fusion.8.refs_0_), channel_id=1, source_target_pairs={{0,16},{8,24},{16,0},{24,8},{1,17},{9,25},{17,1},{25,9},{2,18},{10... | collective-permute-start | bytes 589832 | tf_op jit(solution)/shard_map/ppermute | solution.py:595
  (9 other events, 39.5 us)
where the time goes:
time: 87 us; the launch traced here: 86.9 us
  Pallas kernels  37.7 us (43%)
  starting transfers between devices  28.7 us (33%)
  waiting for transfers between devices  14.7 us (17%)
  other arithmetic  3.56 us (4%)
  local copies, waits for them, and re-layouts  1.37 us (2%)
    ppermute x27, starting transfers between devices, swap(): return lax.ppermute(values, axis, [(i, i ^ bit) for i in range(size)])  28.7 us
    pallas_call x1, Pallas kernels, local_grads(): pl.pallas_call(functools.partial(grads_kernel, sizes), out_shape=[jax.Sha...  26.3 us
    ppermute x27, waiting for transfers between devices, swap(): return lax.ppermute(values, axis, [(i, i ^ bit) for i in range(size)])  14.7 us
    pallas_call x1, Pallas kernels, build_parts(): pl.pallas_call(functools.partial(build_kernel, width - 128), out_shape=[j...  8.05 us
    pallas_call x2, Pallas kernels, update_table(): pl.pallas_call(adagrad_kernel, out_shape=(jax.ShapeDtypeStruct((width, ta...  3.34 us
    convert_element_type x8, other arithmetic, add_half(): (first.astype(jnp.float32) + second.astype(jnp.float32)).astype(jnp.bfloa...  2.24 us
  transfers between devices with their start and end apart: 27, of which 9 were waited for; matrix products, arithmetic and copies ran while one was open for 6% of the time, Pallas kernels for 11%

commit v1 on v0

--- a/solution.py
+++ b/solution.py
@@ -152,14 +152,14 @@
     return jnp.where(matches, 1.0, 0.0).astype(jnp.bfloat16)
 
 
-def place_kernel(shift, owners, ids_ref, home_ref, rank_ref, slot_ref, count_ref):
-    samples, feats = ids_ref.shape
+def place_group(shift, owners, group, ids_ref, home_ref, rank_ref, slot_ref, count_ref):
+    feats = ids_ref.shape[1]
     high, low = home_ref.shape
     half = low // 2
     home = home_ref[...]
     pieces = []
-    for part in (home & 255, home >> 8):
-        down = part.astype(jnp.float32).T
+    for piece in (home & 255, home >> 8):
+        down = piece.astype(jnp.float32).T
         pieces.append(jnp.concatenate([down[:half], down[half:]], axis=1))
     pieces = jnp.concatenate(pieces, axis=0).astype(jnp.bfloat16)
     high_at = lax.broadcasted_iota(jnp.int32, (2 * high, feats), 0)
@@ -167,9 +167,8 @@
     lane = lax.broadcasted_iota(jnp.int32, (1, feats), 1)
     count_lane = lax.broadcasted_iota(jnp.int32, (8, 128), 1)
 
-    @pl.loop(0, samples // 8)
-    def _(group):
-        first = pl.multiple_of(group * 8, 8)
+    for part in range(SAMPLES // 8):
+        first = pl.multiple_of(group * SAMPLES + part * 8, 8)
         ids = ids_ref[pl.ds(first, 8), :]
         every = range(8)
         ones = [ids[row : row + 1] for row in every]
@@ -203,6 +202,7 @@
 
 
 COPY_ROWS = 56
+SAMPLES = 8
 SCRATCH = 16
 
 
@@ -237,15 +237,24 @@
     step = pl.program_id(0)
     outer, inner = positions()
 
+    def place(index):
+        place_group(shift, owners, index, ids_ref, home_ref, rank_ref, slot_ref, found_ref)
+
+    def counts(index):
+        samples = pl.ds(pl.multiple_of(index * group, group), group)
+        return pltpu.make_async_copy(found_ref.at[samples], count_ref.at[samples], copied)
+
     @pl.when(step == 0)
     def _():
-        place_kernel(shift, owners, ids_ref, home_ref, rank_ref, slot_ref, found_ref)
-        copy = pltpu.make_async_copy(found_ref, count_ref, copied)
-        copy.start()
-        copy.wait()
+        place(0)
+        counts(0).start()
 
     @pl.when((step > 0) & (step <= steps))
     def _():
+        counts(step - 1).wait()
+        now = pl.ds(pl.multiple_of((step - 1) * group, group), group)
+        ranks, slots = rank_ref[now, :], slot_ref[now, :]
+        place(jnp.minimum(step, steps - 1))
         gather_rows(
             step - 1,
             outer,
@@ -256,11 +265,15 @@
             mix_ref,
             lift_ref,
             linear_ref,
-            rank_ref,
-            slot_ref,
+            ranks,
+            slots,
             dense_refs,
             *scratch[5:],
         )
+
+        @pl.when(step < steps)
+        def _():
+            counts(step).start()
 
     @pl.when(step > steps)
     def _():
@@ -329,8 +342,8 @@
     mix_ref,
     lift_ref,
     linear_ref,
-    rank_ref,
-    slot_ref,
+    ranks,
+    slots,
     dense_refs,
     mix_down,
     lift_down,
@@ -384,7 +397,7 @@
     ]
     moves, rows_downs = [], []
     for k in every:
-        slot = slot_ref[pl.ds(step * group + k, 1), :]
+        slot = slots[k : k + 1]
         extra = jnp.where(extra_at == 0, slot >> 4, jnp.where(extra_at == 1, slot & 15, 0))
         rows_downs.append(
             jnp.concatenate(
@@ -392,7 +405,7 @@
                 axis=0,
             )
         )
-        moves.append(one_hot(row_at == rank_ref[pl.ds(step * group + k, 1), :]))
+        moves.append(one_hot(row_at == ranks[k : k + 1]))
     for k in every:
         ordered = matmul_nt(moves[k], rows_downs[k])
         sorted_a[now, k, :feats] = ordered[:, :128]
@@ -447,7 +460,7 @@
 def local_grads(x_down, g_down, mix, lift_down, linear, ids, home, owners, part):
     samples, width, feats = x_down.shape
     rank = mix.shape[1]
-    group = 16
+    group = SAMPLES
     steps = samples // group
     per_owner = samples * feats // owners
     far_count = owners // 4

time: 87 us -> 88.9 us (1.022)
  Pallas kernels: 37.7 us -> 39.5 us
    pallas_call x1, Pallas kernels: 26.3 us -> 28.1 us  [local_grads(): pl.pallas_call(functools.partial(grads_kernel, sizes), out_shape=[jax.Sha...]
where the time goes in v1:
time: 88.9 us; the launch traced here: 88.7 us
  Pallas kernels  39.5 us (44%)
  starting transfers between devices  28.8 us (32%)
  waiting for transfers between devices  14.6 us (16%)
  other arithmetic  3.56 us (4%)
  local copies, waits for them, and re-layouts  1.37 us (2%)
    ppermute x27, starting transfers between devices, swap(): return lax.ppermute(values, axis, [(i, i ^ bit) for i in range(size)])  28.8 us
    pallas_call x1, Pallas kernels, local_grads(): pl.pallas_call(functools.partial(grads_kernel, sizes), out_shape=[jax.Sha...  28.1 us
    ppermute x27, waiting for transfers between devices, swap(): return lax.ppermute(values, axis, [(i, i ^ bit) for i in range(size)])  14.6 us
    pallas_call x1, Pallas kernels, build_parts(): pl.pallas_call(functools.partial(build_kernel, width - 128), out_shape=[j...  8.06 us
    pallas_call x2, Pallas kernels, update_table(): pl.pallas_call(adagrad_kernel, out_shape=(jax.ShapeDtypeStruct((width, ta...  3.34 us
    convert_element_type x8, other arithmetic, add_half(): (first.astype(jnp.float32) + second.astype(jnp.float32)).astype(jnp.bfloa...  2.24 us
  transfers between devices with their start and end apart: 27, of which 9 were waited for; matrix products, arithmetic and copies ran while one was open for 6% of the time, Pallas kernels for 11%

profile of v1, /device:TPU:0, one launch (start us, length us, event | category | flops | bytes accessed | tf_op | source)
XLA Modules:
  0.0 88.7 jit_solution(13637386797942911862)
XLA Ops:
  0.6 28.1 %local_grads.1 = (bf16[2,2,192,512]{3,2,1,0:T(8,128)(2,1)}, bf16[2,2,192,512]{3,2,1,0:T(8,128)(2,1)}, bf16[2,2,192,512]{3,2,1,0:T(8,128)(2,1)}, bf16[2,2,192,512...) custom-call(bf16[32,192,256]{2,1,0:T(8,128)(2,1)} %bitcast.129, ...), custom_call_target="tpu_custom_call" | custom-call | flops 12884901888 | bytes 12582912 | tf_op jit(solution)/shard_map/local_grads/pallas_call | solution.py:499
  29.4 2.6 %collective-permute-start.10 = (f32[240,128]{1,0:T(8,128)}, f32[240,128]{1,0:T(8,128)S(1)}, u32[]{:S(2)}, u32[]{:S(2)}) collective-permute-start(f32[240,128]{1,0:T(8,128)} %get-tuple-element.56), channel_id=1, source_target_pairs={{0,24},{8,16},{16,8},{24,0},{1,25},{9,17},{17,9},{25,1},{2,26},{10... | collective-permute-start | bytes 368648 | tf_op jit(solution)/shard_map/ppermute | solution.py:608
  32.5 1.3 %add_convert_fusion.2 = (bf16[1,2,192,512]{3,2,1,0:T(8,128)(2,1)S(1)}, bf16[2,192,512]{2,1,0:T(8,128)(2,1)S(1)}) fusion(bf16[2,2,192,512]{3,2,1,0:T(8,128)(2,1)S(1)} %collective-permute-done, bf16[2,2,192,512]{3,2,1,0:T(8,128)(2,1)} %get-tuple-element.44), kind=kLoop, calls=%fused_computation.2 | loop fusion | flops 1572864 | bytes 2359296 | tf_op jit(solution)/shard_map/convert_element_type | solution.py:612
  33.9 2.0 %collective-permute-start.6 = (bf16[2,192,512]{2,1,0:T(8,128)(2,1)S(1)}, bf16[2,192,512]{2,1,0:T(8,128)(2,1)S(1)}, u32[]{:S(2)}, u32[]{:S(2)}) collective-permute-start(bf16[2,192,512]{2,1,0:T(8,128)(2,1)S(1)} %get-tuple-element.86), channel_id=1, source_target_pairs={{0,1},{1,0},{2,3},{3,2},{4,5},{5,4},{6,7},{7,6},{8,9},{9,8},{10,11... | collective-permute-start | bytes 1179656 | tf_op jit(solution)/shard_map/ppermute | solution.py:608
  36.1 1.6 %collective-permute-start.13 = (bf16[2,192,512]{2,1,0:T(8,128)(2,1)S(1)}, bf16[2,192,512]{2,1,0:T(8,128)(2,1)S(1)}, u32[]{:S(2)}, u32[]{:S(2)}) collective-permute-start(bf16[2,192,512]{2,1,0:T(8,128)(2,1)S(1)} %get-tuple-element.82), channel_id=1, source_target_pairs={{0,16},{8,24},{16,0},{24,8},{1,17},{9,25},{17,1},{25,9},{2,18},{10... | collective-permute-start | bytes 1179656 | tf_op jit(solution)/shard_map/ppermute | solution.py:608
  37.7 8.1 %build_parts.1 = (bf16[2,2,192,512]{3,2,1,0:T(8,128)(2,1)}, bf16[2,2,192,512]{3,2,1,0:T(8,128)(2,1)}, bf16[2,2,192,512]{3,2,1,0:T(8,128)(2,1)}, bf16[2,2,192,512]{3,2,1,0:T(8,128)(2,1)}) custom-call(bf16[4,1024,256]{2,1,0:T(8,128)(2,1)} %get-tuple-element.48.rows_ref), custom_call_target="tpu_custom_call" | custom-call | flops 8589934592 | bytes 6291456 | tf_op jit(solution)/shard_map/build_parts/pallas_call | solution.py:547
  47.3 2.0 %collective-permute-start.14 = (bf16[192,512]{1,0:T(8,128)(2,1)S(1)}, bf16[192,512]{1,0:T(8,128)(2,1)S(1)}, u32[]{:S(2)}, u32[]{:S(2)}) collective-permute-start(bf16[192,512]{1,0:T(8,128)(2,1)S(1)} %fusion.23), channel_id=1, source_target_pairs={{0,1},{1,0},{2,3},{3,2},{4,5},{5,4},{6,7},{7,6},{8,9},{9,8},{10,11... | collective-permute-start | bytes 589832 | tf_op jit(solution)/shard_map/ppermute | solution.py:608
  49.5 1.6 %collective-permute-start.5 = (bf16[2,192,512]{2,1,0:T(8,128)(2,1)S(1)}, bf16[2,192,512]{2,1,0:T(8,128)(2,1)S(1)}, u32[]{:S(2)}, u32[]{:S(2)}) collective-permute-start(bf16[2,192,512]{2,1,0:T(8,128)(2,1)S(1)} %get-tuple-element.84), channel_id=1, source_target_pairs={{0,16},{8,24},{16,0},{24,8},{1,17},{9,25},{17,1},{25,9},{2,18},{10... | collective-permute-start | bytes 1179656 | tf_op jit(solution)/shard_map/ppermute | solution.py:608
  52.0 1.7 %collective-permute-start.16 = (f32[120,128]{1,0:T(8,128)S(1)}, f32[120,128]{1,0:T(8,128)S(1)}, u32[]{:S(2)}, u32[]{:S(2)}) collective-permute-start(f32[120,128]{1,0:T(8,128)S(1)} %bitcast_add_fusion), channel_id=1, source_target_pairs={{0,2},{1,3},{2,0},{3,1},{4,6},{5,7},{6,4},{7,5},{8,10},{9,11},{10,... | collective-permute-start | bytes 184328 | tf_op jit(solution)/shard_map/ppermute | solution.py:608
  53.6 1.3 %collective-permute-done.7 = bf16[192,512]{1,0:T(8,128)(2,1)S(1)} collective-permute-done((bf16[192,512]{1,0:T(8,128)(2,1)S(1)}, bf16[192,512]{1,0:T(8,128)(2,1)S(1)}, u32[]{:S(2)}, u32[]{:S(2)}) %collective-permute-start.7) | collective-permute-done | bytes 196640 | tf_op jit(solution)/shard_map/ppermute | solution.py:608
  55.6 1.6 %collective-permute-start.15 = (bf16[192,512]{1,0:T(8,128)(2,1)S(1)}, bf16[192,512]{1,0:T(8,128)(2,1)S(1)}, u32[]{:S(2)}, u32[]{:S(2)}) collective-permute-start(bf16[192,512]{1,0:T(8,128)(2,1)S(1)} %fusion.14), channel_id=1, source_target_pairs={{0,2},{1,3},{2,0},{3,1},{4,6},{5,7},{6,4},{7,5},{8,10},{9,11},{10,... | collective-permute-start | bytes 589832 | tf_op jit(solution)/shard_map/ppermute | solution.py:608
  57.2 2.7 %collective-permute-start.17 = (f32[120,128]{1,0:T(8,128)S(1)}, f32[120,128]{1,0:T(8,128)S(1)}, u32[]{:S(2)}, u32[]{:S(2)}) collective-permute-start(f32[120,128]{1,0:T(8,128)S(1)} %add.135), channel_id=1, source_target_pairs={{0,4},{1,5},{2,6},{3,7},{4,0},{5,1},{6,2},{7,3},{8,12},{9,13},{10,... | collective-permute-start | bytes 184328 | tf_op jit(solution)/shard_map/ppermute | solution.py:608
  59.9 2.3 %collective-permute-done.5 = bf16[2,192,512]{2,1,0:T(8,128)(2,1)S(1)} collective-permute-done((bf16[2,192,512]{2,1,0:T(8,128)(2,1)S(1)}, bf16[2,192,512]{2,1,0:T(8,128)(2,1)S(1)}, u32[]{:S(2)}, u32[]{:S(2)}) %collective-permute-start.5) | collective-permute-done | bytes 393248 | tf_op jit(solution)/shard_map/ppermute | solution.py:608
  62.2 1.1 %collective-permute-done.4 = bf16[2,192,512]{2,1,0:T(8,128)(2,1)S(1)} collective-permute-done((bf16[2,192,512]{2,1,0:T(8,128)(2,1)S(1)}, bf16[2,192,512]{2,1,0:T(8,128)(2,1)S(1)}, u32[]{:S(2)}, u32[]{:S(2)}) %collective-permute-start.4) | collective-permute-done | bytes 393248 | tf_op jit(solution)/shard_map/ppermute | solution.py:608
  64.4 1.8 %collective-permute-start.12 = (bf16[192,512]{1,0:T(8,128)(2,1)S(1)}, bf16[192,512]{1,0:T(8,128)(2,1)S(1)}, u32[]{:S(2)}, u32[]{:S(2)}) collective-permute-start(bf16[192,512]{1,0:T(8,128)(2,1)S(1)} %get-tuple-element.90), channel_id=1, source_target_pairs={{0,1},{1,0},{2,3},{3,2},{4,5},{5,4},{6,7},{7,6},{8,9},{9,8},{10,11... | collective-permute-start | bytes 589832 | tf_op jit(solution)/shard_map/ppermute | solution.py:608
  66.7 2.6 %collective-permute-start.21 = (bf16[192,512]{1,0:T(8,128)(2,1)S(1)}, bf16[192,512]{1,0:T(8,128)(2,1)S(1)}, u32[]{:S(2)}, u32[]{:S(2)}) collective-permute-start(bf16[192,512]{1,0:T(8,128)(2,1)S(1)} %fusion.10), channel_id=1, source_target_pairs={{0,4},{1,5},{2,6},{3,7},{4,0},{5,1},{6,2},{7,3},{8,12},{9,13},{10,... | collective-permute-start | bytes 589832 | tf_op jit(solution)/shard_map/ppermute | solution.py:608
  69.7 1.7 %collective-permute-start.22 = (bf16[192,512]{1,0:T(8,128)(2,1)S(1)}, bf16[192,512]{1,0:T(8,128)(2,1)S(1)}, u32[]{:S(2)}, u32[]{:S(2)}) collective-permute-start(bf16[192,512]{1,0:T(8,128)(2,1)S(1)} %fusion.5), channel_id=1, source_target_pairs={{0,2},{1,3},{2,0},{3,1},{4,6},{5,7},{6,4},{7,5},{8,10},{9,11},{10,... | collective-permute-start | bytes 589832 | tf_op jit(solution)/shard_map/ppermute | solution.py:608
  71.3 1.6 %collective-permute-start.20 = (f32[2,120,128]{2,1,0:T(8,128)S(1)}, f32[2,120,128]{2,1,0:T(8,128)S(1)}, u32[]{:S(2)}, u32[]{:S(2)}) collective-permute-start(f32[2,120,128]{2,1,0:T(8,128)S(1)} %maximum_select_fusion.3), channel_id=1, source_target_pairs={{0,16},{8,24},{16,0},{24,8},{1,17},{9,25},{17,1},{25,9},{2,18},{10... | collective-permute-start | bytes 368648 | tf_op jit(solution)/shard_map/ppermute | solution.py:608
  72.9 4.0 %collective-permute-done.21 = bf16[192,512]{1,0:T(8,128)(2,1)S(1)} collective-permute-done((bf16[192,512]{1,0:T(8,128)(2,1)S(1)}, bf16[192,512]{1,0:T(8,128)(2,1)S(1)}, u32[]{:S(2)}, u32[]{:S(2)}) %collective-permute-start.21) | collective-permute-done | bytes 196640 | tf_op jit(solution)/shard_map/ppermute | solution.py:608
  78.2 1.0 %collective-permute-start.23 = (bf16[192,512]{1,0:T(8,128)(2,1)S(1)}, bf16[192,512]{1,0:T(8,128)(2,1)S(1)}, u32[]{:S(2)}, u32[]{:S(2)}) collective-permute-start(bf16[192,512]{1,0:T(8,128)(2,1)S(1)} %add_convert_fusion.8.refs_0_), channel_id=1, source_target_pairs={{0,16},{8,24},{16,0},{24,8},{1,17},{9,25},{17,1},{25,9},{2,18},{10... | collective-permute-start | bytes 589832 | tf_op jit(solution)/shard_map/ppermute | solution.py:608
  81.3 1.7 %update_table.2 = (f32[192,2048]{1,0:T(8,128)}, f32[1,2048]{1,0:T(1,128)}) custom-call(s32[2]{0:T(128)S(1)} %pad_add_fusion.me_ref, bf16[192,512]{1,0:T(8,128)(2,1)S(1)} %add_convert_fusion.8.refs_0_, bf16[192,512]{1,0:T(8,128)(2,1)S(1)} %collective-permute-done.24.refs_1_, f32[192,2048]{1,0:T(8,128)S(1)} %bitcast.110, f32[1,2048]{1,0:T(1,128)S(1)} %bitcast.112), custom_call_target="tpu_custom_call" | custom-call | tf_op jit(solution)/shard_map/update_table/pallas_call | solution.py:586
  83.0 2.5 %collective-permute-done.23.refs_0_ = bf16[192,512]{1,0:T(8,128)(2,1)S(1)} collective-permute-done((bf16[192,512]{1,0:T(8,128)(2,1)S(1)}, bf16[192,512]{1,0:T(8,128)(2,1)S(1)}, u32[]{:S(2)}, u32[]{:S(2)}) %collective-permute-start.23) | collective-permute-done | bytes 196640 | tf_op jit(solution)/shard_map/ppermute | solution.py:608
  85.6 1.4 %collective-permute-done.26.refs_1_ = bf16[192,512]{1,0:T(8,128)(2,1)S(1)} collective-permute-done((bf16[192,512]{1,0:T(8,128)(2,1)S(1)}, bf16[192,512]{1,0:T(8,128)(2,1)S(1)}, u32[]{:S(2)}, u32[]{:S(2)}) %collective-permute-start.26) | collective-permute-done | bytes 196640 | tf_op jit(solution)/shard_map/ppermute | solution.py:608
  87.0 1.7 %update_table.3 = (f32[192,2048]{1,0:T(8,128)}, f32[1,2048]{1,0:T(1,128)}) custom-call(s32[2]{0:T(128)S(1)} %pad_add_fusion.me_ref, bf16[192,512]{1,0:T(8,128)(2,1)S(1)} %collective-permute-done.23.refs_0_, bf16[192,512]{1,0:T(8,128)(2,1)S(1)} %collective-permute-done.26.refs_1_, ...), custom_call_target="tpu_custom_call", output_to_operand_aliasing={{0}: (5, {}), {1}: (6, {})} | custom-call | tf_op jit(solution)/shard_map/update_table/pallas_call | solution.py:586
  (73 shorter events, 9.8 us)
Async XLA Ops:
  28.8 3.8 %collective-permute-start = (bf16[2,2,192,512]{3,2,1,0:T(8,128)(2,1)}, bf16[2,2,192,512]{3,2,1,0:T(8,128)(2,1)S(1)}, u32[]{:S(2)}, u32[]{:S(2)}) collective-permute-start(bf16[2,2,192,512]{3,2,1,0:T(8,128)(2,1)} %get-tuple-element.45), channel_id=1, source_target_pairs={{0,8},{8,0},{16,24},{24,16},{1,9},{9,1},{17,25},{25,17},{2,10},{10... | collective-permute-start | bytes 2359304 | tf_op jit(solution)/shard_map/ppermute | solution.py:608
  29.3 6.6 %collective-permute-start.1 = (bf16[2,2,192,512]{3,2,1,0:T(8,128)(2,1)}, bf16[2,2,192,512]{3,2,1,0:T(8,128)(2,1)S(1)}, u32[]{:S(2)}, u32[]{:S(2)}) collective-permute-start(bf16[2,2,192,512]{3,2,1,0:T(8,128)(2,1)} %get-tuple-element.47), channel_id=1, source_target_pairs={{0,8},{8,0},{16,24},{24,16},{1,9},{9,1},{17,25},{25,17},{2,10},{10... | collective-permute-start | bytes 2359304 | tf_op jit(solution)/shard_map/ppermute | solution.py:608
  29.4 16.5 %collective-permute-start.10 = (f32[240,128]{1,0:T(8,128)}, f32[240,128]{1,0:T(8,128)S(1)}, u32[]{:S(2)}, u32[]{:S(2)}) collective-permute-start(f32[240,128]{1,0:T(8,128)} %get-tuple-element.56), channel_id=1, source_target_pairs={{0,24},{8,16},{16,8},{24,0},{1,25},{9,17},{17,9},{25,1},{2,26},{10... | collective-permute-start | bytes 368648 | tf_op jit(solution)/shard_map/ppermute | solution.py:608
  32.0 13.9 %collective-permute-start.8 = (f32[240,128]{1,0:T(8,128)}, f32[240,128]{1,0:T(8,128)S(1)}, u32[]{:S(2)}, u32[]{:S(2)}) collective-permute-start(f32[240,128]{1,0:T(8,128)} %get-tuple-element.54), channel_id=1, source_target_pairs={{0,8},{8,0},{16,24},{24,16},{1,9},{9,1},{17,25},{25,17},{2,10},{10... | collective-permute-start | bytes 368648 | tf_op jit(solution)/shard_map/ppermute | solution.py:608
  32.4 13.5 %collective-permute-start.9 = (f32[240,128]{1,0:T(8,128)}, f32[240,128]{1,0:T(8,128)S(1)}, u32[]{:S(2)}, u32[]{:S(2)}) collective-permute-start(f32[240,128]{1,0:T(8,128)} %get-tuple-element.55), channel_id=1, source_target_pairs={{0,16},{8,24},{16,0},{24,8},{1,17},{9,25},{17,1},{25,9},{2,18},{10... | collective-permute-start | bytes 368648 | tf_op jit(solution)/shard_map/ppermute | solution.py:608
  33.9 13.2 %collective-permute-start.6 = (bf16[2,192,512]{2,1,0:T(8,128)(2,1)S(1)}, bf16[2,192,512]{2,1,0:T(8,128)(2,1)S(1)}, u32[]{:S(2)}, u32[]{:S(2)}) collective-permute-start(bf16[2,192,512]{2,1,0:T(8,128)(2,1)S(1)} %get-tuple-element.86), channel_id=1, source_target_pairs={{0,1},{1,0},{2,3},{3,2},{4,5},{5,4},{6,7},{7,6},{8,9},{9,8},{10,11... | collective-permute-start | bytes 1179656 | tf_op jit(solution)/shard_map/ppermute | solution.py:608
  36.1 11.1 %collective-permute-start.13 = (bf16[2,192,512]{2,1,0:T(8,128)(2,1)S(1)}, bf16[2,192,512]{2,1,0:T(8,128)(2,1)S(1)}, u32[]{:S(2)}, u32[]{:S(2)}) collective-permute-start(bf16[2,192,512]{2,1,0:T(8,128)(2,1)S(1)} %get-tuple-element.82), channel_id=1, source_target_pairs={{0,16},{8,24},{16,0},{24,8},{1,17},{9,25},{17,1},{25,9},{2,18},{10... | collective-permute-start | bytes 1179656 | tf_op jit(solution)/shard_map/ppermute | solution.py:608
  45.8 3.5 %collective-permute-start.2 = (bf16[2,2,192,512]{3,2,1,0:T(8,128)(2,1)}, bf16[2,2,192,512]{3,2,1,0:T(8,128)(2,1)S(1)}, u32[]{:S(2)}, u32[]{:S(2)}) collective-permute-start(bf16[2,2,192,512]{3,2,1,0:T(8,128)(2,1)} %get-tuple-element.50), channel_id=1, source_target_pairs={{0,8},{8,0},{16,24},{24,16},{1,9},{9,1},{17,25},{25,17},{2,10},{10... | collective-permute-start | bytes 2359304 | tf_op jit(solution)/shard_map/ppermute | solution.py:608
  45.9 5.2 %collective-permute-start.3 = (bf16[2,2,192,512]{3,2,1,0:T(8,128)(2,1)}, bf16[2,2,192,512]{3,2,1,0:T(8,128)(2,1)S(1)}, u32[]{:S(2)}, u32[]{:S(2)}) collective-permute-start(bf16[2,2,192,512]{3,2,1,0:T(8,128)(2,1)} %get-tuple-element.52), channel_id=1, source_target_pairs={{0,8},{8,0},{16,24},{24,16},{1,9},{9,1},{17,25},{25,17},{2,10},{10... | collective-permute-start | bytes 2359304 | tf_op jit(solution)/shard_map/ppermute | solution.py:608
  46.5 5.5 %collective-permute-start.11 = (f32[120,128]{1,0:T(8,128)S(1)}, f32[120,128]{1,0:T(8,128)S(1)}, u32[]{:S(2)}, u32[]{:S(2)}) collective-permute-start(f32[120,128]{1,0:T(8,128)S(1)} %dynamic-slice_bitcast_fusion), channel_id=1, source_target_pairs={{0,1},{1,0},{2,3},{3,2},{4,5},{5,4},{6,7},{7,6},{8,9},{9,8},{10,11... | collective-permute-start | bytes 184328 | tf_op jit(solution)/shard_map/ppermute | solution.py:608
  47.1 7.9 %collective-permute-start.7 = (bf16[192,512]{1,0:T(8,128)(2,1)S(1)}, bf16[192,512]{1,0:T(8,128)(2,1)S(1)}, u32[]{:S(2)}, u32[]{:S(2)}) collective-permute-start(bf16[192,512]{1,0:T(8,128)(2,1)S(1)} %fusion.20), channel_id=1, source_target_pairs={{0,16},{8,24},{16,0},{24,8},{1,17},{9,25},{17,1},{25,9},{2,18},{10... | collective-permute-start | bytes 589832 | tf_op jit(solution)/shard_map/ppermute | solution.py:608
  47.3 8.3 %collective-permute-start.14 = (bf16[192,512]{1,0:T(8,128)(2,1)S(1)}, bf16[192,512]{1,0:T(8,128)(2,1)S(1)}, u32[]{:S(2)}, u32[]{:S(2)}) collective-permute-start(bf16[192,512]{1,0:T(8,128)(2,1)S(1)} %fusion.23), channel_id=1, source_target_pairs={{0,1},{1,0},{2,3},{3,2},{4,5},{5,4},{6,7},{7,6},{8,9},{9,8},{10,11... | collective-permute-start | bytes 589832 | tf_op jit(solution)/shard_map/ppermute | solution.py:608
  49.5 12.7 %collective-permute-start.5 = (bf16[2,192,512]{2,1,0:T(8,128)(2,1)S(1)}, bf16[2,192,512]{2,1,0:T(8,128)(2,1)S(1)}, u32[]{:S(2)}, u32[]{:S(2)}) collective-permute-start(bf16[2,192,512]{2,1,0:T(8,128)(2,1)S(1)} %get-tuple-element.84), channel_id=1, source_target_pairs={{0,16},{8,24},{16,0},{24,8},{1,17},{9,25},{17,1},{25,9},{2,18},{10... | collective-permute-start | bytes 1179656 | tf_op jit(solution)/shard_map/ppermute | solution.py:608
  51.3 11.9 %collective-permute-start.4 = (bf16[2,192,512]{2,1,0:T(8,128)(2,1)S(1)}, bf16[2,192,512]{2,1,0:T(8,128)(2,1)S(1)}, u32[]{:S(2)}, u32[]{:S(2)}) collective-permute-start(bf16[2,192,512]{2,1,0:T(8,128)(2,1)S(1)} %get-tuple-element.87), channel_id=1, source_target_pairs={{0,1},{1,0},{2,3},{3,2},{4,5},{5,4},{6,7},{7,6},{8,9},{9,8},{10,11... | collective-permute-start | bytes 1179656 | tf_op jit(solution)/shard_map/ppermute | solution.py:608
  52.0 5.2 %collective-permute-start.16 = (f32[120,128]{1,0:T(8,128)S(1)}, f32[120,128]{1,0:T(8,128)S(1)}, u32[]{:S(2)}, u32[]{:S(2)}) collective-permute-start(f32[120,128]{1,0:T(8,128)S(1)} %bitcast_add_fusion), channel_id=1, source_target_pairs={{0,2},{1,3},{2,0},{3,1},{4,6},{5,7},{6,4},{7,5},{8,10},{9,11},{10,... | collective-permute-start | bytes 184328 | tf_op jit(solution)/shard_map/ppermute | solution.py:608
  55.6 11.0 %collective-permute-start.15 = (bf16[192,512]{1,0:T(8,128)(2,1)S(1)}, bf16[192,512]{1,0:T(8,128)(2,1)S(1)}, u32[]{:S(2)}, u32[]{:S(2)}) collective-permute-start(bf16[192,512]{1,0:T(8,128)(2,1)S(1)} %fusion.14), channel_id=1, source_target_pairs={{0,2},{1,3},{2,0},{3,1},{4,6},{5,7},{6,4},{7,5},{8,10},{9,11},{10,... | collective-permute-start | bytes 589832 | tf_op jit(solution)/shard_map/ppermute | solution.py:608
  57.2 9.0 %collective-permute-start.17 = (f32[120,128]{1,0:T(8,128)S(1)}, f32[120,128]{1,0:T(8,128)S(1)}, u32[]{:S(2)}, u32[]{:S(2)}) collective-permute-start(f32[120,128]{1,0:T(8,128)S(1)} %add.135), channel_id=1, source_target_pairs={{0,4},{1,5},{2,6},{3,7},{4,0},{5,1},{6,2},{7,3},{8,12},{9,13},{10,... | collective-permute-start | bytes 184328 | tf_op jit(solution)/shard_map/ppermute | solution.py:608
  63.3 6.2 %collective-permute-start.19 = (bf16[192,512]{1,0:T(8,128)(2,1)S(1)}, bf16[192,512]{1,0:T(8,128)(2,1)S(1)}, u32[]{:S(2)}, u32[]{:S(2)}) collective-permute-start(bf16[192,512]{1,0:T(8,128)(2,1)S(1)} %fusion.24), channel_id=1, source_target_pairs={{0,16},{8,24},{16,0},{24,8},{1,17},{9,25},{17,1},{25,9},{2,18},{10... | collective-permute-start | bytes 589832 | tf_op jit(solution)/shard_map/ppermute | solution.py:608
  64.4 8.5 %collective-permute-start.12 = (bf16[192,512]{1,0:T(8,128)(2,1)S(1)}, bf16[192,512]{1,0:T(8,128)(2,1)S(1)}, u32[]{:S(2)}, u32[]{:S(2)}) collective-permute-start(bf16[192,512]{1,0:T(8,128)(2,1)S(1)} %get-tuple-element.90), channel_id=1, source_target_pairs={{0,1},{1,0},{2,3},{3,2},{4,5},{5,4},{6,7},{7,6},{8,9},{9,8},{10,11... | collective-permute-start | bytes 589832 | tf_op jit(solution)/shard_map/ppermute | solution.py:608
  66.2 5.1 %collective-permute-start.18 = (f32[120,128]{1,0:T(8,128)S(1)}, f32[120,128]{1,0:T(8,128)S(1)}, u32[]{:S(2)}, u32[]{:S(2)}) collective-permute-start(f32[120,128]{1,0:T(8,128)S(1)} %add.136), channel_id=1, source_target_pairs={{0,1},{1,0},{2,3},{3,2},{4,5},{5,4},{6,7},{7,6},{8,9},{9,8},{10,11... | collective-permute-start | bytes 184328 | tf_op jit(solution)/shard_map/ppermute | solution.py:608
  66.7 10.3 %collective-permute-start.21 = (bf16[192,512]{1,0:T(8,128)(2,1)S(1)}, bf16[192,512]{1,0:T(8,128)(2,1)S(1)}, u32[]{:S(2)}, u32[]{:S(2)}) collective-permute-start(bf16[192,512]{1,0:T(8,128)(2,1)S(1)} %fusion.10), channel_id=1, source_target_pairs={{0,4},{1,5},{2,6},{3,7},{4,0},{5,1},{6,2},{7,3},{8,12},{9,13},{10,... | collective-permute-start | bytes 589832 | tf_op jit(solution)/shard_map/ppermute | solution.py:608
  69.7 8.4 %collective-permute-start.22 = (bf16[192,512]{1,0:T(8,128)(2,1)S(1)}, bf16[192,512]{1,0:T(8,128)(2,1)S(1)}, u32[]{:S(2)}, u32[]{:S(2)}) collective-permute-start(bf16[192,512]{1,0:T(8,128)(2,1)S(1)} %fusion.5), channel_id=1, source_target_pairs={{0,2},{1,3},{2,0},{3,1},{4,6},{5,7},{6,4},{7,5},{8,10},{9,11},{10,... | collective-permute-start | bytes 589832 | tf_op jit(solution)/shard_map/ppermute | solution.py:608
  71.3 5.6 %collective-permute-start.20 = (f32[2,120,128]{2,1,0:T(8,128)S(1)}, f32[2,120,128]{2,1,0:T(8,128)S(1)}, u32[]{:S(2)}, u32[]{:S(2)}) collective-permute-start(f32[2,120,128]{2,1,0:T(8,128)S(1)} %maximum_select_fusion.3), channel_id=1, source_target_pairs={{0,16},{8,24},{16,0},{24,8},{1,17},{9,25},{17,1},{25,9},{2,18},{10... | collective-permute-start | bytes 368648 | tf_op jit(solution)/shard_map/ppermute | solution.py:608
  78.2 7.3 %collective-permute-start.23 = (bf16[192,512]{1,0:T(8,128)(2,1)S(1)}, bf16[192,512]{1,0:T(8,128)(2,1)S(1)}, u32[]{:S(2)}, u32[]{:S(2)}) collective-permute-start(bf16[192,512]{1,0:T(8,128)(2,1)S(1)} %add_convert_fusion.8.refs_0_), channel_id=1, source_target_pairs={{0,16},{8,24},{16,0},{24,8},{1,17},{9,25},{17,1},{25,9},{2,18},{10... | collective-permute-start | bytes 589832 | tf_op jit(solution)/shard_map/ppermute | solution.py:608
  (9 other events, 39.6 us)

commit v2 on v0

--- a/solution.py
+++ b/solution.py
@@ -447,7 +447,7 @@
 def local_grads(x_down, g_down, mix, lift_down, linear, ids, home, owners, part):
     samples, width, feats = x_down.shape
     rank = mix.shape[1]
-    group = 16
+    group = 8
     steps = samples // group
     per_owner = samples * feats // owners
     far_count = owners // 4
@@ -630,12 +630,11 @@
 
     def first_stage(far):
         held = keep[far]
-        if far % 2:
-            parts[far] = add_half(held[1], came[far][1])
-            kept[far] = add_half(held[0], came[far][0])
-        else:
-            parts[far] = add_half(held[:, 1], came[far][:, 1])
-            kept[far] = add_half(held[:, 0], came[far][:, 0])
+        parts[far] = (
+            add_half(held[1], came[far][1]) if far % 2 else add_half(held[:, 1], came[far][:, 1])
+        )
+        held, arrived = after((held, came[far]), parts[far])
+        kept[far] = add_half(held[0], arrived[0]) if far % 2 else add_half(held[:, 0], arrived[:, 0])
 
     def second_stage(far):
         parts[far] = add_half(kept[far][1], sent[far][1])

time: 87 us -> 88.6 us (1.018)
  other arithmetic: 3.56 us -> 5.56 us
    add x1, other arithmetic: 0.03 us -> 1.15 us  [sum_list(): total = total + value]
    convert_element_type x8 -> x12, other arithmetic: 2.24 us -> 3.1 us  [add_half(): (first.astype(jnp.float32) + second.astype(jnp.float32)).astype(jnp.bfloa...]
  transfers between devices with their start and end apart: 27 -> 27, of which waited for: 9 -> 7; matrix products, arithmetic and copies ran while one was open for 6% -> 8% of each run, Pallas kernels for 11% -> 11%
where the time goes in v2:
time: 88.6 us; the launch traced here: 88.4 us
  Pallas kernels  37.8 us (43%)
  starting transfers between devices  28.6 us (32%)
  waiting for transfers between devices  14.1 us (16%)
  other arithmetic  5.56 us (6%)
  local copies, waits for them, and re-layouts  1.38 us (2%)
  between operations  0.89 us (1%)
    ppermute x27, starting transfers between devices, swap(): return lax.ppermute(values, axis, [(i, i ^ bit) for i in range(size)])  28.6 us
    pallas_call x1, Pallas kernels, local_grads(): pl.pallas_call(functools.partial(grads_kernel, sizes), out_shape=[jax.Sha...  26.3 us
    ppermute x27, waiting for transfers between devices, swap(): return lax.ppermute(values, axis, [(i, i ^ bit) for i in range(size)])  14.1 us
    pallas_call x1, Pallas kernels, build_parts(): pl.pallas_call(functools.partial(build_kernel, width - 128), out_shape=[j...  8.15 us
    pallas_call x2, Pallas kernels, update_table(): pl.pallas_call(adagrad_kernel, out_shape=(jax.ShapeDtypeStruct((width, ta...  3.34 us
    convert_element_type x12, other arithmetic, add_half(): (first.astype(jnp.float32) + second.astype(jnp.float32)).astype(jnp.bfloa...  3.1 us
  transfers between devices with their start and end apart: 27, of which 7 were waited for; matrix products, arithmetic and copies ran while one was open for 8% of the time, Pallas kernels for 11%

profile of v2, /device:TPU:0, one launch (start us, length us, event | category | flops | bytes accessed | tf_op | source)
XLA Modules:
  0.0 88.4 jit_solution(9630885655501878786)
XLA Ops:
  0.6 26.3 %local_grads.1 = (bf16[2,2,192,512]{3,2,1,0:T(8,128)(2,1)}, bf16[2,2,192,512]{3,2,1,0:T(8,128)(2,1)}, bf16[2,2,192,512]{3,2,1,0:T(8,128)(2,1)}, bf16[2,2,192,512...) custom-call(bf16[32,192,256]{2,1,0:T(8,128)(2,1)} %bitcast.129, ...), custom_call_target="tpu_custom_call" | custom-call | flops 12884901888 | bytes 12582912 | tf_op jit(solution)/shard_map/local_grads/pallas_call | solution.py:486
  28.0 2.6 %collective-permute-start.9 = (f32[240,128]{1,0:T(8,128)}, f32[240,128]{1,0:T(8,128)}, u32[]{:S(2)}, u32[]{:S(2)}) collective-permute-start(f32[240,128]{1,0:T(8,128)} %get-tuple-element.67), channel_id=1, source_target_pairs={{0,16},{8,24},{16,0},{24,8},{1,17},{9,25},{17,1},{25,9},{2,18},{10... | collective-permute-start | bytes 368648 | tf_op jit(solution)/shard_map/ppermute | solution.py:595
  30.7 1.1 %fusion.1 = bf16[2,192,512]{2,1,0:T(8,128)(2,1)S(1)} fusion(bf16[2,2,192,512]{3,2,1,0:T(8,128)(2,1)S(1)} %collective-permute-done, bf16[2,2,192,512]{3,2,1,0:T(8,128)(2,1)} %get-tuple-element.63), kind=kLoop, calls=%fused_computation.10 | loop fusion | flops 786432 | bytes 1179648 | tf_op jit(solution)/shard_map/convert_element_type | solution.py:599
  31.9 1.8 %collective-permute-start.6 = (bf16[2,192,512]{2,1,0:T(8,128)(2,1)S(1)}, bf16[2,192,512]{2,1,0:T(8,128)(2,1)S(1)}, u32[]{:S(2)}, u32[]{:S(2)}) collective-permute-start(bf16[2,192,512]{2,1,0:T(8,128)(2,1)S(1)} %fusion.1), channel_id=1, source_target_pairs={{0,1},{1,0},{2,3},{3,2},{4,5},{5,4},{6,7},{7,6},{8,9},{9,8},{10,11... | collective-permute-start | bytes 1179656 | tf_op jit(solution)/shard_map/ppermute | solution.py:595
  33.7 1.1 %fusion.2 = bf16[2,192,512]{2,1,0:T(8,128)(2,1)S(1)} fusion(bf16[2,2,192,512]{3,2,1,0:T(8,128)(2,1)S(1)} %collective-permute-done.1, bf16[2,2,192,512]{3,2,1,0:T(8,128)(2,1)} %get-tuple-element.75), kind=kLoop, calls=%fused_computation.11 | loop fusion | flops 786432 | bytes 1179648 | tf_op jit(solution)/shard_map/convert_element_type | solution.py:599
  34.8 1.6 %collective-permute-start.13 = (bf16[2,192,512]{2,1,0:T(8,128)(2,1)S(1)}, bf16[2,192,512]{2,1,0:T(8,128)(2,1)S(1)}, u32[]{:S(2)}, u32[]{:S(2)}) collective-permute-start(bf16[2,192,512]{2,1,0:T(8,128)(2,1)S(1)} %fusion.2), channel_id=1, source_target_pairs={{0,16},{8,24},{16,0},{24,8},{1,17},{9,25},{17,1},{25,9},{2,18},{10... | collective-permute-start | bytes 1179656 | tf_op jit(solution)/shard_map/ppermute | solution.py:595
  36.4 8.2 %build_parts.1 = (bf16[2,2,192,512]{3,2,1,0:T(8,128)(2,1)}, bf16[2,2,192,512]{3,2,1,0:T(8,128)(2,1)}, bf16[2,2,192,512]{3,2,1,0:T(8,128)(2,1)}, bf16[2,2,192,512]{3,2,1,0:T(8,128)(2,1)}) custom-call(bf16[4,1024,256]{2,1,0:T(8,128)(2,1)} %get-tuple-element.56.rows_ref), custom_call_target="tpu_custom_call" | custom-call | flops 8589934592 | bytes 6291456 | tf_op jit(solution)/shard_map/build_parts/pallas_call | solution.py:534
  44.7 1.2 %add_add_fusion = f32[240,128]{1,0:T(8,128)S(1)} fusion(f32[240,128]{1,0:T(8,128)} %collective-permute-done.10, f32[240,128]{1,0:T(8,128)} %collective-permute-done.9, f32[240,128]{1,0:T(8,128)S(1)} %copy-done.6, f32[240,128]{1,0:T(8,128)} %collective-permute-done.8), kind=kLoop, calls=%fused_computation.61 | loop fusion | flops 92160 | bytes 614400 | tf_op jit(solution)/shard_map/add | solution.py:212
  47.4 1.7 %collective-permute-start.14 = (bf16[192,512]{1,0:T(8,128)(2,1)S(1)}, bf16[192,512]{1,0:T(8,128)(2,1)S(1)}, u32[]{:S(2)}, u32[]{:S(2)}) collective-permute-start(bf16[192,512]{1,0:T(8,128)(2,1)S(1)} %fusion.23), channel_id=1, source_target_pairs={{0,1},{1,0},{2,3},{3,2},{4,5},{5,4},{6,7},{7,6},{8,9},{9,8},{10,11... | collective-permute-start | bytes 589832 | tf_op jit(solution)/shard_map/ppermute | solution.py:595
  49.2 1.4 %collective-permute-start.4 = (bf16[2,192,512]{2,1,0:T(8,128)(2,1)S(1)}, bf16[2,192,512]{2,1,0:T(8,128)(2,1)S(1)}, u32[]{:S(2)}, u32[]{:S(2)}) collective-permute-start(bf16[2,192,512]{2,1,0:T(8,128)(2,1)S(1)} %fusion.4), channel_id=1, source_target_pairs={{0,1},{1,0},{2,3},{3,2},{4,5},{5,4},{6,7},{7,6},{8,9},{9,8},{10,11... | collective-permute-start | bytes 1179656 | tf_op jit(solution)/shard_map/ppermute | solution.py:595
  51.5 1.6 %collective-permute-start.16 = (f32[120,128]{1,0:T(8,128)S(1)}, f32[120,128]{1,0:T(8,128)S(1)}, u32[]{:S(2)}, u32[]{:S(2)}) collective-permute-start(f32[120,128]{1,0:T(8,128)S(1)} %bitcast_add_fusion), channel_id=1, source_target_pairs={{0,2},{1,3},{2,0},{3,1},{4,6},{5,7},{6,4},{7,5},{8,10},{9,11},{10,... | collective-permute-start | bytes 184328 | tf_op jit(solution)/shard_map/ppermute | solution.py:595
  53.2 2.0 %collective-permute-done.14 = bf16[192,512]{1,0:T(8,128)(2,1)S(1)} collective-permute-done((bf16[192,512]{1,0:T(8,128)(2,1)S(1)}, bf16[192,512]{1,0:T(8,128)(2,1)S(1)}, u32[]{:S(2)}, u32[]{:S(2)}) %collective-permute-start.14) | collective-permute-done | bytes 196640 | tf_op jit(solution)/shard_map/ppermute | solution.py:595
  55.3 1.8 %collective-permute-start.15 = (bf16[192,512]{1,0:T(8,128)(2,1)S(1)}, bf16[192,512]{1,0:T(8,128)(2,1)S(1)}, u32[]{:S(2)}, u32[]{:S(2)}) collective-permute-start(bf16[192,512]{1,0:T(8,128)(2,1)S(1)} %fusion.14), channel_id=1, source_target_pairs={{0,2},{1,3},{2,0},{3,1},{4,6},{5,7},{6,4},{7,5},{8,10},{9,11},{10,... | collective-permute-start | bytes 589832 | tf_op jit(solution)/shard_map/ppermute | solution.py:595
  57.3 2.7 %collective-permute-start.17 = (f32[120,128]{1,0:T(8,128)S(1)}, f32[120,128]{1,0:T(8,128)S(1)}, u32[]{:S(2)}, u32[]{:S(2)}) collective-permute-start(f32[120,128]{1,0:T(8,128)S(1)} %add.135), channel_id=1, source_target_pairs={{0,4},{1,5},{2,6},{3,7},{4,0},{5,1},{6,2},{7,3},{8,12},{9,13},{10,... | collective-permute-start | bytes 184328 | tf_op jit(solution)/shard_map/ppermute | solution.py:595
  59.9 2.9 %collective-permute-done.4 = bf16[2,192,512]{2,1,0:T(8,128)(2,1)S(1)} collective-permute-done((bf16[2,192,512]{2,1,0:T(8,128)(2,1)S(1)}, bf16[2,192,512]{2,1,0:T(8,128)(2,1)S(1)}, u32[]{:S(2)}, u32[]{:S(2)}) %collective-permute-start.4) | collective-permute-done | bytes 393248 | tf_op jit(solution)/shard_map/ppermute | solution.py:595
  63.0 1.6 %collective-permute-start.19 = (bf16[192,512]{1,0:T(8,128)(2,1)S(1)}, bf16[192,512]{1,0:T(8,128)(2,1)S(1)}, u32[]{:S(2)}, u32[]{:S(2)}) collective-permute-start(bf16[192,512]{1,0:T(8,128)(2,1)S(1)} %fusion.24), channel_id=1, source_target_pairs={{0,16},{8,24},{16,0},{24,8},{1,17},{9,25},{17,1},{25,9},{2,18},{10... | collective-permute-start | bytes 589832 | tf_op jit(solution)/shard_map/ppermute | solution.py:595
  64.6 1.6 %collective-permute-start.12 = (bf16[192,512]{1,0:T(8,128)(2,1)S(1)}, bf16[192,512]{1,0:T(8,128)(2,1)S(1)}, u32[]{:S(2)}, u32[]{:S(2)}) collective-permute-start(bf16[192,512]{1,0:T(8,128)(2,1)S(1)} %get-tuple-element.98), channel_id=1, source_target_pairs={{0,1},{1,0},{2,3},{3,2},{4,5},{5,4},{6,7},{7,6},{8,9},{9,8},{10,11... | collective-permute-start | bytes 589832 | tf_op jit(solution)/shard_map/ppermute | solution.py:595
  66.9 2.6 %collective-permute-start.21 = (bf16[192,512]{1,0:T(8,128)(2,1)S(1)}, bf16[192,512]{1,0:T(8,128)(2,1)S(1)}, u32[]{:S(2)}, u32[]{:S(2)}) collective-permute-start(bf16[192,512]{1,0:T(8,128)(2,1)S(1)} %fusion.10), channel_id=1, source_target_pairs={{0,4},{1,5},{2,6},{3,7},{4,0},{5,1},{6,2},{7,3},{8,12},{9,13},{10,... | collective-permute-start | bytes 589832 | tf_op jit(solution)/shard_map/ppermute | solution.py:595
  69.7 1.7 %collective-permute-start.22 = (bf16[192,512]{1,0:T(8,128)(2,1)S(1)}, bf16[192,512]{1,0:T(8,128)(2,1)S(1)}, u32[]{:S(2)}, u32[]{:S(2)}) collective-permute-start(bf16[192,512]{1,0:T(8,128)(2,1)S(1)} %fusion.5), channel_id=1, source_target_pairs={{0,2},{1,3},{2,0},{3,1},{4,6},{5,7},{6,4},{7,5},{8,10},{9,11},{10,... | collective-permute-start | bytes 589832 | tf_op jit(solution)/shard_map/ppermute | solution.py:595
  72.6 4.8 %collective-permute-done.21 = bf16[192,512]{1,0:T(8,128)(2,1)S(1)} collective-permute-done((bf16[192,512]{1,0:T(8,128)(2,1)S(1)}, bf16[192,512]{1,0:T(8,128)(2,1)S(1)}, u32[]{:S(2)}, u32[]{:S(2)}) %collective-permute-start.21) | collective-permute-done | bytes 196640 | tf_op jit(solution)/shard_map/ppermute | solution.py:595
  81.4 1.7 %update_table.2 = (f32[192,2048]{1,0:T(8,128)}, f32[1,2048]{1,0:T(1,128)}) custom-call(s32[2]{0:T(128)S(1)} %pad_add_fusion.me_ref, bf16[192,512]{1,0:T(8,128)(2,1)S(1)} %add_convert_fusion.8.refs_0_, bf16[192,512]{1,0:T(8,128)(2,1)S(1)} %collective-permute-done.24.refs_1_, f32[192,2048]{1,0:T(8,128)S(1)} %bitcast.110, f32[1,2048]{1,0:T(1,128)S(1)} %bitcast.112), custom_call_target="tpu_custom_call" | custom-call | tf_op jit(solution)/shard_map/update_table/pallas_call | solution.py:573
  83.1 2.2 %collective-permute-done.23.refs_0_ = bf16[192,512]{1,0:T(8,128)(2,1)S(1)} collective-permute-done((bf16[192,512]{1,0:T(8,128)(2,1)S(1)}, bf16[192,512]{1,0:T(8,128)(2,1)S(1)}, u32[]{:S(2)}, u32[]{:S(2)}) %collective-permute-start.23) | collective-permute-done | bytes 196640 | tf_op jit(solution)/shard_map/ppermute | solution.py:595
  85.2 1.4 %collective-permute-done.26.refs_1_ = bf16[192,512]{1,0:T(8,128)(2,1)S(1)} collective-permute-done((bf16[192,512]{1,0:T(8,128)(2,1)S(1)}, bf16[192,512]{1,0:T(8,128)(2,1)S(1)}, u32[]{:S(2)}, u32[]{:S(2)}) %collective-permute-start.26) | collective-permute-done | bytes 196640 | tf_op jit(solution)/shard_map/ppermute | solution.py:595
  86.7 1.7 %update_table.3 = (f32[192,2048]{1,0:T(8,128)}, f32[1,2048]{1,0:T(1,128)}) custom-call(s32[2]{0:T(128)S(1)} %pad_add_fusion.me_ref, bf16[192,512]{1,0:T(8,128)(2,1)S(1)} %collective-permute-done.23.refs_0_, bf16[192,512]{1,0:T(8,128)(2,1)S(1)} %collective-permute-done.26.refs_1_, ...), custom_call_target="tpu_custom_call", output_to_operand_aliasing={{0}: (5, {}), {1}: (6, {})} | custom-call | tf_op jit(solution)/shard_map/update_table/pallas_call | solution.py:573
  (79 shorter events, 10.3 us)
Async XLA Ops:
  27.0 3.8 %collective-permute-start = (bf16[2,2,192,512]{3,2,1,0:T(8,128)(2,1)}, bf16[2,2,192,512]{3,2,1,0:T(8,128)(2,1)S(1)}, u32[]{:S(2)}, u32[]{:S(2)}) collective-permute-start(bf16[2,2,192,512]{3,2,1,0:T(8,128)(2,1)} %get-tuple-element.53), channel_id=1, source_target_pairs={{0,8},{8,0},{16,24},{24,16},{1,9},{9,1},{17,25},{25,17},{2,10},{10... | collective-permute-start | bytes 2359304 | tf_op jit(solution)/shard_map/ppermute | solution.py:595
  27.5 6.2 %collective-permute-start.1 = (bf16[2,2,192,512]{3,2,1,0:T(8,128)(2,1)}, bf16[2,2,192,512]{3,2,1,0:T(8,128)(2,1)S(1)}, u32[]{:S(2)}, u32[]{:S(2)}) collective-permute-start(bf16[2,2,192,512]{3,2,1,0:T(8,128)(2,1)} %get-tuple-element.55), channel_id=1, source_target_pairs={{0,8},{8,0},{16,24},{24,16},{1,9},{9,1},{17,25},{25,17},{2,10},{10... | collective-permute-start | bytes 2359304 | tf_op jit(solution)/shard_map/ppermute | solution.py:595
  27.6 17.0 %collective-permute-start.8 = (f32[240,128]{1,0:T(8,128)}, f32[240,128]{1,0:T(8,128)}, u32[]{:S(2)}, u32[]{:S(2)}) collective-permute-start(f32[240,128]{1,0:T(8,128)} %get-tuple-element.66), channel_id=1, source_target_pairs={{0,8},{8,0},{16,24},{24,16},{1,9},{9,1},{17,25},{25,17},{2,10},{10... | collective-permute-start | bytes 368648 | tf_op jit(solution)/shard_map/ppermute | solution.py:595
  28.0 16.6 %collective-permute-start.9 = (f32[240,128]{1,0:T(8,128)}, f32[240,128]{1,0:T(8,128)}, u32[]{:S(2)}, u32[]{:S(2)}) collective-permute-start(f32[240,128]{1,0:T(8,128)} %get-tuple-element.67), channel_id=1, source_target_pairs={{0,16},{8,24},{16,0},{24,8},{1,17},{9,25},{17,1},{25,9},{2,18},{10... | collective-permute-start | bytes 368648 | tf_op jit(solution)/shard_map/ppermute | solution.py:595
  30.6 14.0 %collective-permute-start.10 = (f32[240,128]{1,0:T(8,128)}, f32[240,128]{1,0:T(8,128)}, u32[]{:S(2)}, u32[]{:S(2)}) collective-permute-start(f32[240,128]{1,0:T(8,128)} %get-tuple-element.68), channel_id=1, source_target_pairs={{0,24},{8,16},{16,8},{24,0},{1,25},{9,17},{17,9},{25,1},{2,26},{10... | collective-permute-start | bytes 368648 | tf_op jit(solution)/shard_map/ppermute | solution.py:595
  31.9 15.0 %collective-permute-start.6 = (bf16[2,192,512]{2,1,0:T(8,128)(2,1)S(1)}, bf16[2,192,512]{2,1,0:T(8,128)(2,1)S(1)}, u32[]{:S(2)}, u32[]{:S(2)}) collective-permute-start(bf16[2,192,512]{2,1,0:T(8,128)(2,1)S(1)} %fusion.1), channel_id=1, source_target_pairs={{0,1},{1,0},{2,3},{3,2},{4,5},{5,4},{6,7},{7,6},{8,9},{9,8},{10,11... | collective-permute-start | bytes 1179656 | tf_op jit(solution)/shard_map/ppermute | solution.py:595
  34.8 12.5 %collective-permute-start.13 = (bf16[2,192,512]{2,1,0:T(8,128)(2,1)S(1)}, bf16[2,192,512]{2,1,0:T(8,128)(2,1)S(1)}, u32[]{:S(2)}, u32[]{:S(2)}) collective-permute-start(bf16[2,192,512]{2,1,0:T(8,128)(2,1)S(1)} %fusion.2), channel_id=1, source_target_pairs={{0,16},{8,24},{16,0},{24,8},{1,17},{9,25},{17,1},{25,9},{2,18},{10... | collective-permute-start | bytes 1179656 | tf_op jit(solution)/shard_map/ppermute | solution.py:595
  44.5 6.1 %collective-permute-start.2 = (bf16[2,2,192,512]{3,2,1,0:T(8,128)(2,1)}, bf16[2,2,192,512]{3,2,1,0:T(8,128)(2,1)S(1)}, u32[]{:S(2)}, u32[]{:S(2)}) collective-permute-start(bf16[2,2,192,512]{3,2,1,0:T(8,128)(2,1)} %get-tuple-element.58), channel_id=1, source_target_pairs={{0,8},{8,0},{16,24},{24,16},{1,9},{9,1},{17,25},{25,17},{2,10},{10... | collective-permute-start | bytes 2359304 | tf_op jit(solution)/shard_map/ppermute | solution.py:595
  45.8 5.7 %collective-permute-start.11 = (f32[120,128]{1,0:T(8,128)S(1)}, f32[120,128]{1,0:T(8,128)S(1)}, u32[]{:S(2)}, u32[]{:S(2)}) collective-permute-start(f32[120,128]{1,0:T(8,128)S(1)} %dynamic-slice_bitcast_fusion), channel_id=1, source_target_pairs={{0,1},{1,0},{2,3},{3,2},{4,5},{5,4},{6,7},{7,6},{8,9},{9,8},{10,11... | collective-permute-start | bytes 184328 | tf_op jit(solution)/shard_map/ppermute | solution.py:595
  46.9 8.3 %collective-permute-start.7 = (bf16[192,512]{1,0:T(8,128)(2,1)S(1)}, bf16[192,512]{1,0:T(8,128)(2,1)S(1)}, u32[]{:S(2)}, u32[]{:S(2)}) collective-permute-start(bf16[192,512]{1,0:T(8,128)(2,1)S(1)} %fusion.20), channel_id=1, source_target_pairs={{0,16},{8,24},{16,0},{24,8},{1,17},{9,25},{17,1},{25,9},{2,18},{10... | collective-permute-start | bytes 589832 | tf_op jit(solution)/shard_map/ppermute | solution.py:595
  47.4 7.8 %collective-permute-start.14 = (bf16[192,512]{1,0:T(8,128)(2,1)S(1)}, bf16[192,512]{1,0:T(8,128)(2,1)S(1)}, u32[]{:S(2)}, u32[]{:S(2)}) collective-permute-start(bf16[192,512]{1,0:T(8,128)(2,1)S(1)} %fusion.23), channel_id=1, source_target_pairs={{0,1},{1,0},{2,3},{3,2},{4,5},{5,4},{6,7},{7,6},{8,9},{9,8},{10,11... | collective-permute-start | bytes 589832 | tf_op jit(solution)/shard_map/ppermute | solution.py:595
  49.2 13.7 %collective-permute-start.4 = (bf16[2,192,512]{2,1,0:T(8,128)(2,1)S(1)}, bf16[2,192,512]{2,1,0:T(8,128)(2,1)S(1)}, u32[]{:S(2)}, u32[]{:S(2)}) collective-permute-start(bf16[2,192,512]{2,1,0:T(8,128)(2,1)S(1)} %fusion.4), channel_id=1, source_target_pairs={{0,1},{1,0},{2,3},{3,2},{4,5},{5,4},{6,7},{7,6},{8,9},{9,8},{10,11... | collective-permute-start | bytes 1179656 | tf_op jit(solution)/shard_map/ppermute | solution.py:595
  50.7 12.2 %collective-permute-start.5 = (bf16[2,192,512]{2,1,0:T(8,128)(2,1)S(1)}, bf16[2,192,512]{2,1,0:T(8,128)(2,1)S(1)}, u32[]{:S(2)}, u32[]{:S(2)}) collective-permute-start(bf16[2,192,512]{2,1,0:T(8,128)(2,1)S(1)} %fusion.3), channel_id=1, source_target_pairs={{0,16},{8,24},{16,0},{24,8},{1,17},{9,25},{17,1},{25,9},{2,18},{10... | collective-permute-start | bytes 1179656 | tf_op jit(solution)/shard_map/ppermute | solution.py:595
  51.5 5.7 %collective-permute-start.16 = (f32[120,128]{1,0:T(8,128)S(1)}, f32[120,128]{1,0:T(8,128)S(1)}, u32[]{:S(2)}, u32[]{:S(2)}) collective-permute-start(f32[120,128]{1,0:T(8,128)S(1)} %bitcast_add_fusion), channel_id=1, source_target_pairs={{0,2},{1,3},{2,0},{3,1},{4,6},{5,7},{6,4},{7,5},{8,10},{9,11},{10,... | collective-permute-start | bytes 184328 | tf_op jit(solution)/shard_map/ppermute | solution.py:595
  55.3 10.9 %collective-permute-start.15 = (bf16[192,512]{1,0:T(8,128)(2,1)S(1)}, bf16[192,512]{1,0:T(8,128)(2,1)S(1)}, u32[]{:S(2)}, u32[]{:S(2)}) collective-permute-start(bf16[192,512]{1,0:T(8,128)(2,1)S(1)} %fusion.14), channel_id=1, source_target_pairs={{0,2},{1,3},{2,0},{3,1},{4,6},{5,7},{6,4},{7,5},{8,10},{9,11},{10,... | collective-permute-start | bytes 589832 | tf_op jit(solution)/shard_map/ppermute | solution.py:595
  57.3 8.9 %collective-permute-start.17 = (f32[120,128]{1,0:T(8,128)S(1)}, f32[120,128]{1,0:T(8,128)S(1)}, u32[]{:S(2)}, u32[]{:S(2)}) collective-permute-start(f32[120,128]{1,0:T(8,128)S(1)} %add.135), channel_id=1, source_target_pairs={{0,4},{1,5},{2,6},{3,7},{4,0},{5,1},{6,2},{7,3},{8,12},{9,13},{10,... | collective-permute-start | bytes 184328 | tf_op jit(solution)/shard_map/ppermute | solution.py:595
  63.0 6.6 %collective-permute-start.19 = (bf16[192,512]{1,0:T(8,128)(2,1)S(1)}, bf16[192,512]{1,0:T(8,128)(2,1)S(1)}, u32[]{:S(2)}, u32[]{:S(2)}) collective-permute-start(bf16[192,512]{1,0:T(8,128)(2,1)S(1)} %fusion.24), channel_id=1, source_target_pairs={{0,16},{8,24},{16,0},{24,8},{1,17},{9,25},{17,1},{25,9},{2,18},{10... | collective-permute-start | bytes 589832 | tf_op jit(solution)/shard_map/ppermute | solution.py:595
  64.6 7.9 %collective-permute-start.12 = (bf16[192,512]{1,0:T(8,128)(2,1)S(1)}, bf16[192,512]{1,0:T(8,128)(2,1)S(1)}, u32[]{:S(2)}, u32[]{:S(2)}) collective-permute-start(bf16[192,512]{1,0:T(8,128)(2,1)S(1)} %get-tuple-element.98), channel_id=1, source_target_pairs={{0,1},{1,0},{2,3},{3,2},{4,5},{5,4},{6,7},{7,6},{8,9},{9,8},{10,11... | collective-permute-start | bytes 589832 | tf_op jit(solution)/shard_map/ppermute | solution.py:595
  66.2 5.5 %collective-permute-start.18 = (f32[120,128]{1,0:T(8,128)S(1)}, f32[120,128]{1,0:T(8,128)S(1)}, u32[]{:S(2)}, u32[]{:S(2)}) collective-permute-start(f32[120,128]{1,0:T(8,128)S(1)} %add.136), channel_id=1, source_target_pairs={{0,1},{1,0},{2,3},{3,2},{4,5},{5,4},{6,7},{7,6},{8,9},{9,8},{10,11... | collective-permute-start | bytes 184328 | tf_op jit(solution)/shard_map/ppermute | solution.py:595
  66.9 10.4 %collective-permute-start.21 = (bf16[192,512]{1,0:T(8,128)(2,1)S(1)}, bf16[192,512]{1,0:T(8,128)(2,1)S(1)}, u32[]{:S(2)}, u32[]{:S(2)}) collective-permute-start(bf16[192,512]{1,0:T(8,128)(2,1)S(1)} %fusion.10), channel_id=1, source_target_pairs={{0,4},{1,5},{2,6},{3,7},{4,0},{5,1},{6,2},{7,3},{8,12},{9,13},{10,... | collective-permute-start | bytes 589832 | tf_op jit(solution)/shard_map/ppermute | solution.py:595
  69.7 8.1 %collective-permute-start.22 = (bf16[192,512]{1,0:T(8,128)(2,1)S(1)}, bf16[192,512]{1,0:T(8,128)(2,1)S(1)}, u32[]{:S(2)}, u32[]{:S(2)}) collective-permute-start(bf16[192,512]{1,0:T(8,128)(2,1)S(1)} %fusion.5), channel_id=1, source_target_pairs={{0,2},{1,3},{2,0},{3,1},{4,6},{5,7},{6,4},{7,5},{8,10},{9,11},{10,... | collective-permute-start | bytes 589832 | tf_op jit(solution)/shard_map/ppermute | solution.py:595
  71.8 5.6 %collective-permute-start.20 = (f32[2,120,128]{2,1,0:T(8,128)S(1)}, f32[2,120,128]{2,1,0:T(8,128)S(1)}, u32[]{:S(2)}, u32[]{:S(2)}) collective-permute-start(f32[2,120,128]{2,1,0:T(8,128)S(1)} %maximum_select_fusion.3), channel_id=1, source_target_pairs={{0,16},{8,24},{16,0},{24,8},{1,17},{9,25},{17,1},{25,9},{2,18},{10... | collective-permute-start | bytes 368648 | tf_op jit(solution)/shard_map/ppermute | solution.py:595
  77.9 3.5 %collective-permute-start.24 = (bf16[192,512]{1,0:T(8,128)(2,1)S(1)}, bf16[192,512]{1,0:T(8,128)(2,1)S(1)}, u32[]{:S(2)}, u32[]{:S(2)}) collective-permute-start(bf16[192,512]{1,0:T(8,128)(2,1)S(1)} %add_convert_fusion.8.refs_0_), channel_id=1, source_target_pairs={{0,8},{8,0},{16,24},{24,16},{1,9},{9,1},{17,25},{25,17},{2,10},{10... | collective-permute-start | bytes 589832 | tf_op jit(solution)/shard_map/ppermute | solution.py:595
  78.2 7.1 %collective-permute-start.23 = (bf16[192,512]{1,0:T(8,128)(2,1)S(1)}, bf16[192,512]{1,0:T(8,128)(2,1)S(1)}, u32[]{:S(2)}, u32[]{:S(2)}) collective-permute-start(bf16[192,512]{1,0:T(8,128)(2,1)S(1)} %add_convert_fusion.8.refs_0_), channel_id=1, source_target_pairs={{0,16},{8,24},{16,0},{24,8},{1,17},{9,25},{17,1},{25,9},{2,18},{10... | collective-permute-start | bytes 589832 | tf_op jit(solution)/shard_map/ppermute | solution.py:595
  (10 other events, 43.3 us)

commit v3 on v0

--- a/solution.py
+++ b/solution.py
@@ -203,7 +203,7 @@
 
 
 COPY_ROWS = 56
-SCRATCH = 16
+SCRATCH = 19
 
 
 def sum_list(values):
@@ -233,33 +233,50 @@
     keep_refs, send_refs = rest[:far_count], rest[far_count : 2 * far_count]
     rows_ref = rest[2 * far_count]
     dense_refs, scratch = rest[2 * far_count + 1 : -SCRATCH], rest[-SCRATCH:]
-    rank_ref, slot_ref, found_ref, count_ref, copied = scratch[:5]
+    rank_ref, slot_ref, found_ref, count_ref, copied, x_held, g_held, landed = scratch[:8]
     step = pl.program_id(0)
     outer, inner = positions()
 
+    def fetch(index):
+        samples, slot = pl.ds(pl.multiple_of(index * group, group), group), index % 2
+        return [
+            pltpu.make_async_copy(ref.at[samples], held.at[slot], landed.at[at, slot])
+            for at, (ref, held) in enumerate(((x_ref, x_held), (g_ref, g_held)))
+        ]
+
     @pl.when(step == 0)
     def _():
+        for copy in fetch(0):
+            copy.start()
         place_kernel(shift, owners, ids_ref, home_ref, rank_ref, slot_ref, found_ref)
         copy = pltpu.make_async_copy(found_ref, count_ref, copied)
         copy.start()
         copy.wait()
 
+    @pl.when((step > 0) & (step < steps))
+    def _():
+        for copy in fetch(step):
+            copy.start()
+
     @pl.when((step > 0) & (step <= steps))
     def _():
+        for copy in fetch(step - 1):
+            copy.wait()
+        slot = (step - 1) % 2
         gather_rows(
             step - 1,
             outer,
             sizes,
             count_ref,
-            x_ref,
-            g_ref,
+            x_held.at[slot],
+            g_held.at[slot],
             mix_ref,
             lift_ref,
             linear_ref,
             rank_ref,
             slot_ref,
             dense_refs,
-            *scratch[5:],
+            *scratch[8:],
         )
 
     @pl.when(step > steps)
@@ -270,9 +287,9 @@
         rows_ref[0, :, :128] = row_a[near, pl.ds(0, per_owner), :].astype(jnp.bfloat16)
         rows_ref[0, :, 128:] = row_b[near, pl.ds(0, per_owner), :].astype(jnp.bfloat16)
         owner = place ^ inner
-        first_rows = row_a[owner, pl.ds(0, per_owner), :]
-        second_rows = row_b[owner, pl.ds(0, per_owner), :]
-        at = x_ref.shape[1] - 128
+        first_rows = row_a[owner, pl.ds(0, per_owner), :].astype(jnp.bfloat16)
+        second_rows = row_b[owner, pl.ds(0, per_owner), :].astype(jnp.bfloat16)
+        at = x_held.shape[2] - 128
         build_rows(at, outer, first_rows, second_rows, place, far_count, keep_refs, send_refs)
 
 
@@ -417,8 +434,9 @@
 def build_rows(at, my_outer, first_rows, second_rows, place, first, keep_refs, send_refs):
     outers, piece = 2 * keep_refs[0].shape[1], keep_refs[0].shape[3]
     per_owner = first_rows.shape[0]
-    rows_down = jnp.concatenate([first_rows.T, second_rows.T[:at]], axis=0).astype(jnp.bfloat16)
-    slots = second_rows[:, at : at + 1] * 16.0 + second_rows[:, at + 1 : at + 2]
+    rows_down = jnp.concatenate([first_rows.T, second_rows.T[:at]], axis=0)
+    slots = second_rows.astype(jnp.float32)
+    slots = slots[:, at : at + 1] * 16.0 + slots[:, at + 1 : at + 2]
     slots = slots.astype(jnp.int32)
     lanes = lax.broadcasted_iota(jnp.int32, (per_owner, piece), 1)
     totals = []
@@ -457,9 +475,7 @@
     def whole(shape):
         return pl.BlockSpec(shape, lambda i, *_: (0,) * len(shape))
 
-    sample_spec = pl.BlockSpec(
-        (group, width, feats), lambda i: (jnp.clip(i - 1, 0, steps - 1), 0, 0)
-    )
+    sample_spec = pl.BlockSpec(memory_space=pl.ANY)
     dense_rows = feats * (1 + feats // 128) + width
     outers = 2 * part[1]
     dense_piece = (dense_rows // outers, 128)
@@ -471,6 +487,9 @@
         pltpu.VMEM((samples, 128), jnp.int32),
         pltpu.SMEM((samples, 128), jnp.int32),
         pltpu.SemaphoreType.DMA,
+        pltpu.VMEM((2, group, width, feats), jnp.bfloat16),
+        pltpu.VMEM((2, group, width, feats), jnp.bfloat16),
+        pltpu.SemaphoreType.DMA((2, 2)),
         pltpu.VMEM((rank, feats), jnp.bfloat16),
         pltpu.VMEM((rank, width), jnp.bfloat16),
         pltpu.VMEM((feats, rank), jnp.float32),
@@ -521,7 +540,7 @@
 
 def build_kernel(at, rows_ref, *refs):
     half = len(refs) // 2
-    rows = rows_ref[0].astype(jnp.float32)
+    rows = rows_ref[0]
     place = 2 * half - 1 - pl.program_id(0)
     keep_refs, send_refs = refs[:half], refs[half:]
     outer, _ = positions()

time: 87 us -> 86.1 us (0.990)
  Pallas kernels: 37.7 us -> 36.5 us
    pallas_call x1, Pallas kernels: 26.3 us -> 25.2 us  [local_grads(): pl.pallas_call(functools.partial(grads_kernel, sizes), out_shape=[jax.Sha...]
where the time goes in v3:
time: 86.1 us; the launch traced here: 85.9 us
  Pallas kernels  36.5 us (42%)
  starting transfers between devices  28.8 us (33%)
  waiting for transfers between devices  14.8 us (17%)
  other arithmetic  3.56 us (4%)
  local copies, waits for them, and re-layouts  1.37 us (2%)
    ppermute x27, starting transfers between devices, swap(): return lax.ppermute(values, axis, [(i, i ^ bit) for i in range(size)])  28.8 us
    pallas_call x1, Pallas kernels, local_grads(): pl.pallas_call(functools.partial(grads_kernel, sizes), out_shape=[jax.Sha...  25.2 us
    ppermute x27, waiting for transfers between devices, swap(): return lax.ppermute(values, axis, [(i, i ^ bit) for i in range(size)])  14.8 us
    pallas_call x1, Pallas kernels, build_parts(): pl.pallas_call(functools.partial(build_kernel, width - 128), out_shape=[j...  7.98 us
    pallas_call x2, Pallas kernels, update_table(): pl.pallas_call(adagrad_kernel, out_shape=(jax.ShapeDtypeStruct((width, ta...  3.34 us
    convert_element_type x8, other arithmetic, add_half(): (first.astype(jnp.float32) + second.astype(jnp.float32)).astype(jnp.bfloa...  2.24 us
  transfers between devices with their start and end apart: 27, of which 9 were waited for; matrix products, arithmetic and copies ran while one was open for 6% of the time, Pallas kernels for 11%

profile of v3, /device:TPU:0, one launch (start us, length us, event | category | flops | bytes accessed | tf_op | source)
XLA Modules:
  0.0 85.9 jit_solution(210763161878487796)
XLA Ops:
  0.6 25.2 %local_grads.1 = (bf16[2,2,192,512]{3,2,1,0:T(8,128)(2,1)}, bf16[2,2,192,512]{3,2,1,0:T(8,128)(2,1)}, bf16[2,2,192,512]{3,2,1,0:T(8,128)(2,1)}, bf16[2,2,192,512...) custom-call(bf16[32,192,256]{2,1,0:T(8,128)(2,1)} %bitcast.129, ...), custom_call_target="tpu_custom_call" | custom-call | flops 12884901888 | bytes 12582912 | tf_op jit(solution)/shard_map/local_grads/pallas_call | solution.py:505
  26.4 2.6 %collective-permute-start.10 = (f32[240,128]{1,0:T(8,128)}, f32[240,128]{1,0:T(8,128)S(1)}, u32[]{:S(2)}, u32[]{:S(2)}) collective-permute-start(f32[240,128]{1,0:T(8,128)} %get-tuple-element.56), channel_id=1, source_target_pairs={{0,24},{8,16},{16,8},{24,0},{1,25},{9,17},{17,9},{25,1},{2,26},{10... | collective-permute-start | bytes 368648 | tf_op jit(solution)/shard_map/ppermute | solution.py:614
  29.6 1.3 %add_convert_fusion.2 = (bf16[1,2,192,512]{3,2,1,0:T(8,128)(2,1)S(1)}, bf16[2,192,512]{2,1,0:T(8,128)(2,1)S(1)}) fusion(bf16[2,2,192,512]{3,2,1,0:T(8,128)(2,1)S(1)} %collective-permute-done, bf16[2,2,192,512]{3,2,1,0:T(8,128)(2,1)} %get-tuple-element.44), kind=kLoop, calls=%fused_computation.2 | loop fusion | flops 1572864 | bytes 2359296 | tf_op jit(solution)/shard_map/convert_element_type | solution.py:618
  30.9 2.0 %collective-permute-start.6 = (bf16[2,192,512]{2,1,0:T(8,128)(2,1)S(1)}, bf16[2,192,512]{2,1,0:T(8,128)(2,1)S(1)}, u32[]{:S(2)}, u32[]{:S(2)}) collective-permute-start(bf16[2,192,512]{2,1,0:T(8,128)(2,1)S(1)} %get-tuple-element.86), channel_id=1, source_target_pairs={{0,1},{1,0},{2,3},{3,2},{4,5},{5,4},{6,7},{7,6},{8,9},{9,8},{10,11... | collective-permute-start | bytes 1179656 | tf_op jit(solution)/shard_map/ppermute | solution.py:614
  33.2 1.6 %collective-permute-start.13 = (bf16[2,192,512]{2,1,0:T(8,128)(2,1)S(1)}, bf16[2,192,512]{2,1,0:T(8,128)(2,1)S(1)}, u32[]{:S(2)}, u32[]{:S(2)}) collective-permute-start(bf16[2,192,512]{2,1,0:T(8,128)(2,1)S(1)} %get-tuple-element.82), channel_id=1, source_target_pairs={{0,16},{8,24},{16,0},{24,8},{1,17},{9,25},{17,1},{25,9},{2,18},{10... | collective-permute-start | bytes 1179656 | tf_op jit(solution)/shard_map/ppermute | solution.py:614
  34.8 8.0 %build_parts.1 = (bf16[2,2,192,512]{3,2,1,0:T(8,128)(2,1)}, bf16[2,2,192,512]{3,2,1,0:T(8,128)(2,1)}, bf16[2,2,192,512]{3,2,1,0:T(8,128)(2,1)}, bf16[2,2,192,512]{3,2,1,0:T(8,128)(2,1)}) custom-call(bf16[4,1024,256]{2,1,0:T(8,128)(2,1)} %get-tuple-element.48.rows_ref), custom_call_target="tpu_custom_call" | custom-call | flops 8589934592 | bytes 6291456 | tf_op jit(solution)/shard_map/build_parts/pallas_call | solution.py:553
  44.3 2.1 %collective-permute-start.14 = (bf16[192,512]{1,0:T(8,128)(2,1)S(1)}, bf16[192,512]{1,0:T(8,128)(2,1)S(1)}, u32[]{:S(2)}, u32[]{:S(2)}) collective-permute-start(bf16[192,512]{1,0:T(8,128)(2,1)S(1)} %fusion.23), channel_id=1, source_target_pairs={{0,1},{1,0},{2,3},{3,2},{4,5},{5,4},{6,7},{7,6},{8,9},{9,8},{10,11... | collective-permute-start | bytes 589832 | tf_op jit(solution)/shard_map/ppermute | solution.py:614
  46.6 1.6 %collective-permute-start.5 = (bf16[2,192,512]{2,1,0:T(8,128)(2,1)S(1)}, bf16[2,192,512]{2,1,0:T(8,128)(2,1)S(1)}, u32[]{:S(2)}, u32[]{:S(2)}) collective-permute-start(bf16[2,192,512]{2,1,0:T(8,128)(2,1)S(1)} %get-tuple-element.84), channel_id=1, source_target_pairs={{0,16},{8,24},{16,0},{24,8},{1,17},{9,25},{17,1},{25,9},{2,18},{10... | collective-permute-start | bytes 1179656 | tf_op jit(solution)/shard_map/ppermute | solution.py:614
  49.0 1.7 %collective-permute-start.16 = (f32[120,128]{1,0:T(8,128)S(1)}, f32[120,128]{1,0:T(8,128)S(1)}, u32[]{:S(2)}, u32[]{:S(2)}) collective-permute-start(f32[120,128]{1,0:T(8,128)S(1)} %bitcast_add_fusion), channel_id=1, source_target_pairs={{0,2},{1,3},{2,0},{3,1},{4,6},{5,7},{6,4},{7,5},{8,10},{9,11},{10,... | collective-permute-start | bytes 184328 | tf_op jit(solution)/shard_map/ppermute | solution.py:614
  50.7 1.3 %collective-permute-done.7 = bf16[192,512]{1,0:T(8,128)(2,1)S(1)} collective-permute-done((bf16[192,512]{1,0:T(8,128)(2,1)S(1)}, bf16[192,512]{1,0:T(8,128)(2,1)S(1)}, u32[]{:S(2)}, u32[]{:S(2)}) %collective-permute-start.7) | collective-permute-done | bytes 196640 | tf_op jit(solution)/shard_map/ppermute | solution.py:614
  52.6 1.7 %collective-permute-start.15 = (bf16[192,512]{1,0:T(8,128)(2,1)S(1)}, bf16[192,512]{1,0:T(8,128)(2,1)S(1)}, u32[]{:S(2)}, u32[]{:S(2)}) collective-permute-start(bf16[192,512]{1,0:T(8,128)(2,1)S(1)} %fusion.14), channel_id=1, source_target_pairs={{0,2},{1,3},{2,0},{3,1},{4,6},{5,7},{6,4},{7,5},{8,10},{9,11},{10,... | collective-permute-start | bytes 589832 | tf_op jit(solution)/shard_map/ppermute | solution.py:614
  54.3 2.6 %collective-permute-start.17 = (f32[120,128]{1,0:T(8,128)S(1)}, f32[120,128]{1,0:T(8,128)S(1)}, u32[]{:S(2)}, u32[]{:S(2)}) collective-permute-start(f32[120,128]{1,0:T(8,128)S(1)} %add.135), channel_id=1, source_target_pairs={{0,4},{1,5},{2,6},{3,7},{4,0},{5,1},{6,2},{7,3},{8,12},{9,13},{10,... | collective-permute-start | bytes 184328 | tf_op jit(solution)/shard_map/ppermute | solution.py:614
  56.9 2.3 %collective-permute-done.5 = bf16[2,192,512]{2,1,0:T(8,128)(2,1)S(1)} collective-permute-done((bf16[2,192,512]{2,1,0:T(8,128)(2,1)S(1)}, bf16[2,192,512]{2,1,0:T(8,128)(2,1)S(1)}, u32[]{:S(2)}, u32[]{:S(2)}) %collective-permute-start.5) | collective-permute-done | bytes 393248 | tf_op jit(solution)/shard_map/ppermute | solution.py:614
  59.2 1.1 %collective-permute-done.4 = bf16[2,192,512]{2,1,0:T(8,128)(2,1)S(1)} collective-permute-done((bf16[2,192,512]{2,1,0:T(8,128)(2,1)S(1)}, bf16[2,192,512]{2,1,0:T(8,128)(2,1)S(1)}, u32[]{:S(2)}, u32[]{:S(2)}) %collective-permute-start.4) | collective-permute-done | bytes 393248 | tf_op jit(solution)/shard_map/ppermute | solution.py:614
  61.5 1.8 %collective-permute-start.12 = (bf16[192,512]{1,0:T(8,128)(2,1)S(1)}, bf16[192,512]{1,0:T(8,128)(2,1)S(1)}, u32[]{:S(2)}, u32[]{:S(2)}) collective-permute-start(bf16[192,512]{1,0:T(8,128)(2,1)S(1)} %get-tuple-element.90), channel_id=1, source_target_pairs={{0,1},{1,0},{2,3},{3,2},{4,5},{5,4},{6,7},{7,6},{8,9},{9,8},{10,11... | collective-permute-start | bytes 589832 | tf_op jit(solution)/shard_map/ppermute | solution.py:614
  63.7 2.7 %collective-permute-start.21 = (bf16[192,512]{1,0:T(8,128)(2,1)S(1)}, bf16[192,512]{1,0:T(8,128)(2,1)S(1)}, u32[]{:S(2)}, u32[]{:S(2)}) collective-permute-start(bf16[192,512]{1,0:T(8,128)(2,1)S(1)} %fusion.10), channel_id=1, source_target_pairs={{0,4},{1,5},{2,6},{3,7},{4,0},{5,1},{6,2},{7,3},{8,12},{9,13},{10,... | collective-permute-start | bytes 589832 | tf_op jit(solution)/shard_map/ppermute | solution.py:614
  66.8 1.6 %collective-permute-start.22 = (bf16[192,512]{1,0:T(8,128)(2,1)S(1)}, bf16[192,512]{1,0:T(8,128)(2,1)S(1)}, u32[]{:S(2)}, u32[]{:S(2)}) collective-permute-start(bf16[192,512]{1,0:T(8,128)(2,1)S(1)} %fusion.5), channel_id=1, source_target_pairs={{0,2},{1,3},{2,0},{3,1},{4,6},{5,7},{6,4},{7,5},{8,10},{9,11},{10,... | collective-permute-start | bytes 589832 | tf_op jit(solution)/shard_map/ppermute | solution.py:614
  68.4 1.6 %collective-permute-start.20 = (f32[2,120,128]{2,1,0:T(8,128)S(1)}, f32[2,120,128]{2,1,0:T(8,128)S(1)}, u32[]{:S(2)}, u32[]{:S(2)}) collective-permute-start(f32[2,120,128]{2,1,0:T(8,128)S(1)} %maximum_select_fusion.3), channel_id=1, source_target_pairs={{0,16},{8,24},{16,0},{24,8},{1,17},{9,25},{17,1},{25,9},{2,18},{10... | collective-permute-start | bytes 368648 | tf_op jit(solution)/shard_map/ppermute | solution.py:614
  70.1 3.9 %collective-permute-done.21 = bf16[192,512]{1,0:T(8,128)(2,1)S(1)} collective-permute-done((bf16[192,512]{1,0:T(8,128)(2,1)S(1)}, bf16[192,512]{1,0:T(8,128)(2,1)S(1)}, u32[]{:S(2)}, u32[]{:S(2)}) %collective-permute-start.21) | collective-permute-done | bytes 196640 | tf_op jit(solution)/shard_map/ppermute | solution.py:614
  74.2 1.1 %collective-permute-done.22 = bf16[192,512]{1,0:T(8,128)(2,1)S(1)} collective-permute-done((bf16[192,512]{1,0:T(8,128)(2,1)S(1)}, bf16[192,512]{1,0:T(8,128)(2,1)S(1)}, u32[]{:S(2)}, u32[]{:S(2)}) %collective-permute-start.22) | collective-permute-done | bytes 196640 | tf_op jit(solution)/shard_map/ppermute | solution.py:614
  78.5 1.7 %update_table.2 = (f32[192,2048]{1,0:T(8,128)}, f32[1,2048]{1,0:T(1,128)}) custom-call(s32[2]{0:T(128)S(1)} %pad_add_fusion.me_ref, bf16[192,512]{1,0:T(8,128)(2,1)S(1)} %add_convert_fusion.8.refs_0_, bf16[192,512]{1,0:T(8,128)(2,1)S(1)} %collective-permute-done.24.refs_1_, f32[192,2048]{1,0:T(8,128)S(1)} %bitcast.110, f32[1,2048]{1,0:T(1,128)S(1)} %bitcast.112), custom_call_target="tpu_custom_call" | custom-call | tf_op jit(solution)/shard_map/update_table/pallas_call | solution.py:592
  80.1 2.6 %collective-permute-done.23.refs_0_ = bf16[192,512]{1,0:T(8,128)(2,1)S(1)} collective-permute-done((bf16[192,512]{1,0:T(8,128)(2,1)S(1)}, bf16[192,512]{1,0:T(8,128)(2,1)S(1)}, u32[]{:S(2)}, u32[]{:S(2)}) %collective-permute-start.23) | collective-permute-done | bytes 196640 | tf_op jit(solution)/shard_map/ppermute | solution.py:614
  82.8 1.4 %collective-permute-done.26.refs_1_ = bf16[192,512]{1,0:T(8,128)(2,1)S(1)} collective-permute-done((bf16[192,512]{1,0:T(8,128)(2,1)S(1)}, bf16[192,512]{1,0:T(8,128)(2,1)S(1)}, u32[]{:S(2)}, u32[]{:S(2)}) %collective-permute-start.26) | collective-permute-done | bytes 196640 | tf_op jit(solution)/shard_map/ppermute | solution.py:614
  84.2 1.7 %update_table.3 = (f32[192,2048]{1,0:T(8,128)}, f32[1,2048]{1,0:T(1,128)}) custom-call(s32[2]{0:T(128)S(1)} %pad_add_fusion.me_ref, bf16[192,512]{1,0:T(8,128)(2,1)S(1)} %collective-permute-done.23.refs_0_, bf16[192,512]{1,0:T(8,128)(2,1)S(1)} %collective-permute-done.26.refs_1_, ...), custom_call_target="tpu_custom_call", output_to_operand_aliasing={{0}: (5, {}), {1}: (6, {})} | custom-call | tf_op jit(solution)/shard_map/update_table/pallas_call | solution.py:592
  (73 shorter events, 9.8 us)
Async XLA Ops:
  25.8 3.8 %collective-permute-start = (bf16[2,2,192,512]{3,2,1,0:T(8,128)(2,1)}, bf16[2,2,192,512]{3,2,1,0:T(8,128)(2,1)S(1)}, u32[]{:S(2)}, u32[]{:S(2)}) collective-permute-start(bf16[2,2,192,512]{3,2,1,0:T(8,128)(2,1)} %get-tuple-element.45), channel_id=1, source_target_pairs={{0,8},{8,0},{16,24},{24,16},{1,9},{9,1},{17,25},{25,17},{2,10},{10... | collective-permute-start | bytes 2359304 | tf_op jit(solution)/shard_map/ppermute | solution.py:614
  26.3 6.6 %collective-permute-start.1 = (bf16[2,2,192,512]{3,2,1,0:T(8,128)(2,1)}, bf16[2,2,192,512]{3,2,1,0:T(8,128)(2,1)S(1)}, u32[]{:S(2)}, u32[]{:S(2)}) collective-permute-start(bf16[2,2,192,512]{3,2,1,0:T(8,128)(2,1)} %get-tuple-element.47), channel_id=1, source_target_pairs={{0,8},{8,0},{16,24},{24,16},{1,9},{9,1},{17,25},{25,17},{2,10},{10... | collective-permute-start | bytes 2359304 | tf_op jit(solution)/shard_map/ppermute | solution.py:614
  26.4 16.4 %collective-permute-start.10 = (f32[240,128]{1,0:T(8,128)}, f32[240,128]{1,0:T(8,128)S(1)}, u32[]{:S(2)}, u32[]{:S(2)}) collective-permute-start(f32[240,128]{1,0:T(8,128)} %get-tuple-element.56), channel_id=1, source_target_pairs={{0,24},{8,16},{16,8},{24,0},{1,25},{9,17},{17,9},{25,1},{2,26},{10... | collective-permute-start | bytes 368648 | tf_op jit(solution)/shard_map/ppermute | solution.py:614
  29.1 13.8 %collective-permute-start.8 = (f32[240,128]{1,0:T(8,128)}, f32[240,128]{1,0:T(8,128)S(1)}, u32[]{:S(2)}, u32[]{:S(2)}) collective-permute-start(f32[240,128]{1,0:T(8,128)} %get-tuple-element.54), channel_id=1, source_target_pairs={{0,8},{8,0},{16,24},{24,16},{1,9},{9,1},{17,25},{25,17},{2,10},{10... | collective-permute-start | bytes 368648 | tf_op jit(solution)/shard_map/ppermute | solution.py:614
  29.5 13.4 %collective-permute-start.9 = (f32[240,128]{1,0:T(8,128)}, f32[240,128]{1,0:T(8,128)S(1)}, u32[]{:S(2)}, u32[]{:S(2)}) collective-permute-start(f32[240,128]{1,0:T(8,128)} %get-tuple-element.55), channel_id=1, source_target_pairs={{0,16},{8,24},{16,0},{24,8},{1,17},{9,25},{17,1},{25,9},{2,18},{10... | collective-permute-start | bytes 368648 | tf_op jit(solution)/shard_map/ppermute | solution.py:614
  30.9 13.1 %collective-permute-start.6 = (bf16[2,192,512]{2,1,0:T(8,128)(2,1)S(1)}, bf16[2,192,512]{2,1,0:T(8,128)(2,1)S(1)}, u32[]{:S(2)}, u32[]{:S(2)}) collective-permute-start(bf16[2,192,512]{2,1,0:T(8,128)(2,1)S(1)} %get-tuple-element.86), channel_id=1, source_target_pairs={{0,1},{1,0},{2,3},{3,2},{4,5},{5,4},{6,7},{7,6},{8,9},{9,8},{10,11... | collective-permute-start | bytes 1179656 | tf_op jit(solution)/shard_map/ppermute | solution.py:614
  33.2 11.0 %collective-permute-start.13 = (bf16[2,192,512]{2,1,0:T(8,128)(2,1)S(1)}, bf16[2,192,512]{2,1,0:T(8,128)(2,1)S(1)}, u32[]{:S(2)}, u32[]{:S(2)}) collective-permute-start(bf16[2,192,512]{2,1,0:T(8,128)(2,1)S(1)} %get-tuple-element.82), channel_id=1, source_target_pairs={{0,16},{8,24},{16,0},{24,8},{1,17},{9,25},{17,1},{25,9},{2,18},{10... | collective-permute-start | bytes 1179656 | tf_op jit(solution)/shard_map/ppermute | solution.py:614
  42.8 3.6 %collective-permute-start.2 = (bf16[2,2,192,512]{3,2,1,0:T(8,128)(2,1)}, bf16[2,2,192,512]{3,2,1,0:T(8,128)(2,1)S(1)}, u32[]{:S(2)}, u32[]{:S(2)}) collective-permute-start(bf16[2,2,192,512]{3,2,1,0:T(8,128)(2,1)} %get-tuple-element.50), channel_id=1, source_target_pairs={{0,8},{8,0},{16,24},{24,16},{1,9},{9,1},{17,25},{25,17},{2,10},{10... | collective-permute-start | bytes 2359304 | tf_op jit(solution)/shard_map/ppermute | solution.py:614
  42.9 5.3 %collective-permute-start.3 = (bf16[2,2,192,512]{3,2,1,0:T(8,128)(2,1)}, bf16[2,2,192,512]{3,2,1,0:T(8,128)(2,1)S(1)}, u32[]{:S(2)}, u32[]{:S(2)}) collective-permute-start(bf16[2,2,192,512]{3,2,1,0:T(8,128)(2,1)} %get-tuple-element.52), channel_id=1, source_target_pairs={{0,8},{8,0},{16,24},{24,16},{1,9},{9,1},{17,25},{25,17},{2,10},{10... | collective-permute-start | bytes 2359304 | tf_op jit(solution)/shard_map/ppermute | solution.py:614
  43.4 5.6 %collective-permute-start.11 = (f32[120,128]{1,0:T(8,128)S(1)}, f32[120,128]{1,0:T(8,128)S(1)}, u32[]{:S(2)}, u32[]{:S(2)}) collective-permute-start(f32[120,128]{1,0:T(8,128)S(1)} %dynamic-slice_bitcast_fusion), channel_id=1, source_target_pairs={{0,1},{1,0},{2,3},{3,2},{4,5},{5,4},{6,7},{7,6},{8,9},{9,8},{10,11... | collective-permute-start | bytes 184328 | tf_op jit(solution)/shard_map/ppermute | solution.py:614
  44.1 7.9 %collective-permute-start.7 = (bf16[192,512]{1,0:T(8,128)(2,1)S(1)}, bf16[192,512]{1,0:T(8,128)(2,1)S(1)}, u32[]{:S(2)}, u32[]{:S(2)}) collective-permute-start(bf16[192,512]{1,0:T(8,128)(2,1)S(1)} %fusion.20), channel_id=1, source_target_pairs={{0,16},{8,24},{16,0},{24,8},{1,17},{9,25},{17,1},{25,9},{2,18},{10... | collective-permute-start | bytes 589832 | tf_op jit(solution)/shard_map/ppermute | solution.py:614
  44.3 8.3 %collective-permute-start.14 = (bf16[192,512]{1,0:T(8,128)(2,1)S(1)}, bf16[192,512]{1,0:T(8,128)(2,1)S(1)}, u32[]{:S(2)}, u32[]{:S(2)}) collective-permute-start(bf16[192,512]{1,0:T(8,128)(2,1)S(1)} %fusion.23), channel_id=1, source_target_pairs={{0,1},{1,0},{2,3},{3,2},{4,5},{5,4},{6,7},{7,6},{8,9},{9,8},{10,11... | collective-permute-start | bytes 589832 | tf_op jit(solution)/shard_map/ppermute | solution.py:614
  46.6 12.6 %collective-permute-start.5 = (bf16[2,192,512]{2,1,0:T(8,128)(2,1)S(1)}, bf16[2,192,512]{2,1,0:T(8,128)(2,1)S(1)}, u32[]{:S(2)}, u32[]{:S(2)}) collective-permute-start(bf16[2,192,512]{2,1,0:T(8,128)(2,1)S(1)} %get-tuple-element.84), channel_id=1, source_target_pairs={{0,16},{8,24},{16,0},{24,8},{1,17},{9,25},{17,1},{25,9},{2,18},{10... | collective-permute-start | bytes 1179656 | tf_op jit(solution)/shard_map/ppermute | solution.py:614
  48.4 12.0 %collective-permute-start.4 = (bf16[2,192,512]{2,1,0:T(8,128)(2,1)S(1)}, bf16[2,192,512]{2,1,0:T(8,128)(2,1)S(1)}, u32[]{:S(2)}, u32[]{:S(2)}) collective-permute-start(bf16[2,192,512]{2,1,0:T(8,128)(2,1)S(1)} %get-tuple-element.87), channel_id=1, source_target_pairs={{0,1},{1,0},{2,3},{3,2},{4,5},{5,4},{6,7},{7,6},{8,9},{9,8},{10,11... | collective-permute-start | bytes 1179656 | tf_op jit(solution)/shard_map/ppermute | solution.py:614
  49.0 5.3 %collective-permute-start.16 = (f32[120,128]{1,0:T(8,128)S(1)}, f32[120,128]{1,0:T(8,128)S(1)}, u32[]{:S(2)}, u32[]{:S(2)}) collective-permute-start(f32[120,128]{1,0:T(8,128)S(1)} %bitcast_add_fusion), channel_id=1, source_target_pairs={{0,2},{1,3},{2,0},{3,1},{4,6},{5,7},{6,4},{7,5},{8,10},{9,11},{10,... | collective-permute-start | bytes 184328 | tf_op jit(solution)/shard_map/ppermute | solution.py:614
  52.6 11.0 %collective-permute-start.15 = (bf16[192,512]{1,0:T(8,128)(2,1)S(1)}, bf16[192,512]{1,0:T(8,128)(2,1)S(1)}, u32[]{:S(2)}, u32[]{:S(2)}) collective-permute-start(bf16[192,512]{1,0:T(8,128)(2,1)S(1)} %fusion.14), channel_id=1, source_target_pairs={{0,2},{1,3},{2,0},{3,1},{4,6},{5,7},{6,4},{7,5},{8,10},{9,11},{10,... | collective-permute-start | bytes 589832 | tf_op jit(solution)/shard_map/ppermute | solution.py:614
  54.3 9.0 %collective-permute-start.17 = (f32[120,128]{1,0:T(8,128)S(1)}, f32[120,128]{1,0:T(8,128)S(1)}, u32[]{:S(2)}, u32[]{:S(2)}) collective-permute-start(f32[120,128]{1,0:T(8,128)S(1)} %add.135), channel_id=1, source_target_pairs={{0,4},{1,5},{2,6},{3,7},{4,0},{5,1},{6,2},{7,3},{8,12},{9,13},{10,... | collective-permute-start | bytes 184328 | tf_op jit(solution)/shard_map/ppermute | solution.py:614
  60.4 6.3 %collective-permute-start.19 = (bf16[192,512]{1,0:T(8,128)(2,1)S(1)}, bf16[192,512]{1,0:T(8,128)(2,1)S(1)}, u32[]{:S(2)}, u32[]{:S(2)}) collective-permute-start(bf16[192,512]{1,0:T(8,128)(2,1)S(1)} %fusion.24), channel_id=1, source_target_pairs={{0,16},{8,24},{16,0},{24,8},{1,17},{9,25},{17,1},{25,9},{2,18},{10... | collective-permute-start | bytes 589832 | tf_op jit(solution)/shard_map/ppermute | solution.py:614
  61.5 8.6 %collective-permute-start.12 = (bf16[192,512]{1,0:T(8,128)(2,1)S(1)}, bf16[192,512]{1,0:T(8,128)(2,1)S(1)}, u32[]{:S(2)}, u32[]{:S(2)}) collective-permute-start(bf16[192,512]{1,0:T(8,128)(2,1)S(1)} %get-tuple-element.90), channel_id=1, source_target_pairs={{0,1},{1,0},{2,3},{3,2},{4,5},{5,4},{6,7},{7,6},{8,9},{9,8},{10,11... | collective-permute-start | bytes 589832 | tf_op jit(solution)/shard_map/ppermute | solution.py:614
  63.3 5.1 %collective-permute-start.18 = (f32[120,128]{1,0:T(8,128)S(1)}, f32[120,128]{1,0:T(8,128)S(1)}, u32[]{:S(2)}, u32[]{:S(2)}) collective-permute-start(f32[120,128]{1,0:T(8,128)S(1)} %add.136), channel_id=1, source_target_pairs={{0,1},{1,0},{2,3},{3,2},{4,5},{5,4},{6,7},{7,6},{8,9},{9,8},{10,11... | collective-permute-start | bytes 184328 | tf_op jit(solution)/shard_map/ppermute | solution.py:614
  63.7 10.3 %collective-permute-start.21 = (bf16[192,512]{1,0:T(8,128)(2,1)S(1)}, bf16[192,512]{1,0:T(8,128)(2,1)S(1)}, u32[]{:S(2)}, u32[]{:S(2)}) collective-permute-start(bf16[192,512]{1,0:T(8,128)(2,1)S(1)} %fusion.10), channel_id=1, source_target_pairs={{0,4},{1,5},{2,6},{3,7},{4,0},{5,1},{6,2},{7,3},{8,12},{9,13},{10,... | collective-permute-start | bytes 589832 | tf_op jit(solution)/shard_map/ppermute | solution.py:614
  66.8 8.5 %collective-permute-start.22 = (bf16[192,512]{1,0:T(8,128)(2,1)S(1)}, bf16[192,512]{1,0:T(8,128)(2,1)S(1)}, u32[]{:S(2)}, u32[]{:S(2)}) collective-permute-start(bf16[192,512]{1,0:T(8,128)(2,1)S(1)} %fusion.5), channel_id=1, source_target_pairs={{0,2},{1,3},{2,0},{3,1},{4,6},{5,7},{6,4},{7,5},{8,10},{9,11},{10,... | collective-permute-start | bytes 589832 | tf_op jit(solution)/shard_map/ppermute | solution.py:614
  68.4 5.6 %collective-permute-start.20 = (f32[2,120,128]{2,1,0:T(8,128)S(1)}, f32[2,120,128]{2,1,0:T(8,128)S(1)}, u32[]{:S(2)}, u32[]{:S(2)}) collective-permute-start(f32[2,120,128]{2,1,0:T(8,128)S(1)} %maximum_select_fusion.3), channel_id=1, source_target_pairs={{0,16},{8,24},{16,0},{24,8},{1,17},{9,25},{17,1},{25,9},{2,18},{10... | collective-permute-start | bytes 368648 | tf_op jit(solution)/shard_map/ppermute | solution.py:614
  75.5 7.3 %collective-permute-start.23 = (bf16[192,512]{1,0:T(8,128)(2,1)S(1)}, bf16[192,512]{1,0:T(8,128)(2,1)S(1)}, u32[]{:S(2)}, u32[]{:S(2)}) collective-permute-start(bf16[192,512]{1,0:T(8,128)(2,1)S(1)} %add_convert_fusion.8.refs_0_), channel_id=1, source_target_pairs={{0,16},{8,24},{16,0},{24,8},{1,17},{9,25},{17,1},{25,9},{2,18},{10... | collective-permute-start | bytes 589832 | tf_op jit(solution)/shard_map/ppermute | solution.py:614
  (9 other events, 39.8 us)
